TPU v7x, 32 devices: a whole 2x2x4 slice. The times are simulated.
32 devices in a mesh: fsdp: 16 (over z, x, core), rep: 2 (over y).
Axes of the slice: x: 2, y: 2, z: 4, core: 2. Of those that a mesh axis runs over, the one named last changes fastest.
Arguments:
- tokens: bfloat16 [49152, 768], P(('fsdp', 'rep')), may hold values from -6 to 6
- segments: int32 [192, 256], P(('fsdp', 'rep')), may hold values from 0 to 3, never falling along the last dimension, each value on 1 to 128 neighbouring positions
- cotangent: bfloat16 [49152, 768], P(('fsdp', 'rep')), may hold values from -6 to 6
- attn_gain: bfloat16 [768], P(('fsdp', 'rep')), may hold values from 0.25 to 1.75
- attn_shift: bfloat16 [768], P(('fsdp', 'rep')), may hold values from -3 to 3
- qkv_weight: bfloat16 [768, 2304], P(('fsdp', 'rep')), may hold values from -0.21875 to 0.21875
- query_bias: bfloat16 [768], P(('fsdp', 'rep')), may hold values from -3 to 3
- value_bias: bfloat16 [768], P(('fsdp', 'rep')), may hold values from -3 to 3
- out_weight: bfloat16 [768, 768], P(('fsdp', 'rep')), may hold values from -1.25 to 1.25
- out_bias: bfloat16 [768], P(('fsdp', 'rep')), may hold values from -3 to 3
- mlp_gain: bfloat16 [768], P(('fsdp', 'rep')), may hold values from 0.25 to 1.75
- mlp_shift: bfloat16 [768], P(('fsdp', 'rep')), may hold values from -3 to 3
- up_weight: bfloat16 [768, 3072], P(('fsdp', 'rep')), may hold values from -0.21875 to 0.21875
- up_bias: bfloat16 [3072], P(('fsdp', 'rep')), may hold values from -3 to 3
- down_weight: bfloat16 [3072, 768], P(('fsdp', 'rep')), may hold values from -0.15625 to 0.15625
- down_bias: bfloat16 [768], P(('fsdp', 'rep')), may hold values from -3 to 3
Outputs:
- out: bfloat16 [49152, 768], P(('fsdp', 'rep'))
- grad_tokens: float32 [49152, 768], P(('fsdp', 'rep'))
- grad_attn_gain: float32 [768], P(('fsdp', 'rep'))
- grad_attn_shift: float32 [768], P(('fsdp', 'rep'))
- grad_qkv_weight: float32 [768, 2304], P(('fsdp', 'rep'))
- grad_query_bias: float32 [768], P(('fsdp', 'rep'))
- grad_value_bias: float32 [768], P(('fsdp', 'rep'))
- grad_out_weight: float32 [768, 768], P(('fsdp', 'rep'))
- grad_out_bias: float32 [768], P(('fsdp', 'rep'))
- grad_mlp_gain: float32 [768], P(('fsdp', 'rep'))
- grad_mlp_shift: float32 [768], P(('fsdp', 'rep'))
- grad_up_weight: float32 [768, 3072], P(('fsdp', 'rep'))
- grad_up_bias: float32 [3072], P(('fsdp', 'rep'))
- grad_down_weight: float32 [3072, 768], P(('fsdp', 'rep'))
- grad_down_bias: float32 [768], P(('fsdp', 'rep'))
Inputs may be any that keep to these rules, and one draw needn't show every extreme that they name: `segments`: within each sequence the numbers never fall; each of the 4 documents has 1 to 128 tokens, one exactly 128.
All inputs are finite; a program needn't handle non-finite values.
Results may differ from a plain program's by a relative error of at most 0.011.
Values may be sent and summed in bfloat16 or wider, within the bound.
A program may use at most 192 MiB of HBM per device.

v0:
```python
import math

import jax
import jax.numpy as jnp
from jax import lax
from jax.sharding import PartitionSpec as P

D = 768
HEADS = 12
LEN = 256


EPSILON = 1e-05


def norm_rows(values, gain, shift):
    center = values - jnp.mean(values, axis=-1, keepdims=True)
    spread = jnp.mean(center * center, axis=-1, keepdims=True)
    return center * lax.rsqrt(spread + EPSILON) * gain + shift


def gelu_tanh(values):
    return (
        0.5
        * values
        * (1.0 + jnp.tanh(0.7978845608028654 * (values + 0.044715 * values * values * values)))
    )


def block_mask(seg_block):
    places = jnp.arange(seg_block.shape[1])
    causal = places[None, :] <= places[:, None]
    same_doc = seg_block[:, :, None] == seg_block[:, None, :]
    return jnp.logical_and(same_doc, causal[None])


def masked_scores(queries, key_rows, allowed, score_scale):
    raw = jnp.einsum("sqhd,skhd->shqk", queries, key_rows, preferred_element_type=jnp.float32)
    return jnp.where(allowed[:, None], raw * score_scale, -1e30)


def local(
    tokens,
    segments,
    cotangent,
    attn_gain,
    attn_shift,
    qkv_weight,
    query_bias,
    value_bias,
    out_weight,
    out_bias,
    mlp_gain,
    mlp_shift,
    up_weight,
    up_bias,
    down_weight,
    down_bias,
):
    gathered = (
        lax.all_gather(attn_gain, ("fsdp", "rep"), axis=0, tiled=True),
        lax.all_gather(attn_shift, ("fsdp", "rep"), axis=0, tiled=True),
        lax.all_gather(qkv_weight, ("fsdp", "rep"), axis=0, tiled=True),
        lax.all_gather(query_bias, ("fsdp", "rep"), axis=0, tiled=True),
        lax.all_gather(value_bias, ("fsdp", "rep"), axis=0, tiled=True),
        lax.all_gather(out_weight, ("fsdp", "rep"), axis=0, tiled=True),
        lax.all_gather(out_bias, ("fsdp", "rep"), axis=0, tiled=True),
        lax.all_gather(mlp_gain, ("fsdp", "rep"), axis=0, tiled=True),
        lax.all_gather(mlp_shift, ("fsdp", "rep"), axis=0, tiled=True),
        lax.all_gather(up_weight, ("fsdp", "rep"), axis=0, tiled=True),
        lax.all_gather(up_bias, ("fsdp", "rep"), axis=0, tiled=True),
        lax.all_gather(down_weight, ("fsdp", "rep"), axis=0, tiled=True),
        lax.all_gather(down_bias, ("fsdp", "rep"), axis=0, tiled=True),
    )
    (
        gain_attn,
        shift_attn,
        mat_qkv,
        bias_query,
        bias_value,
        mat_out,
        bias_out,
        gain_mlp,
        shift_mlp,
        mat_up,
        bias_up,
        mat_down,
        bias_down,
    ) = gathered
    f32 = jnp.float32
    low16 = jnp.bfloat16
    seq_count = segments.shape[0]
    seq_span = min(seq_count, max(1, 512 // LEN))
    block_count = seq_count // seq_span
    head_dim = D // HEADS
    score_scale = 1.0 / math.sqrt(head_dim)
    rows_in = tokens.astype(f32)
    normed16 = norm_rows(rows_in, gain_attn.astype(f32), shift_attn.astype(f32)).astype(low16)
    qkv_bias = jnp.concatenate(
        [bias_query.astype(f32), jnp.zeros((D,), f32), bias_value.astype(f32)]
    )
    qkv16 = (jnp.dot(normed16, mat_qkv, preferred_element_type=f32) + qkv_bias).astype(low16)
    heads_view = qkv16.reshape(seq_count, LEN, 3, HEADS, head_dim)
    attn_parts = []
    lse_parts = []
    for number in range(block_count):
        first_seq = number * seq_span
        current = heads_view[first_seq : first_seq + seq_span]
        allowed = block_mask(segments[first_seq : first_seq + seq_span])
        scores = masked_scores(current[:, :, 0], current[:, :, 1], allowed, score_scale)
        row_max = jnp.max(scores, axis=-1, keepdims=True)
        exponent = jnp.exp(scores - row_max)
        totals = jnp.sum(exponent, axis=-1, keepdims=True)
        probs_low = (exponent / totals).astype(low16)
        lse_parts.append(row_max + jnp.log(totals))
        mixed = jnp.einsum(
            "shqk,skhd->sqhd", probs_low, current[:, :, 2], preferred_element_type=f32
        )
        attn_parts.append(mixed.reshape(seq_span * LEN, D))
    attended16 = jnp.concatenate(attn_parts, axis=0).astype(low16)
    branch = jnp.dot(attended16, mat_out, preferred_element_type=f32) + bias_out.astype(f32)
    resid = rows_in + branch
    normed_mlp16 = norm_rows(resid, gain_mlp.astype(f32), shift_mlp.astype(f32)).astype(low16)
    hidden_pre = jnp.dot(normed_mlp16, mat_up, preferred_element_type=f32) + bias_up.astype(f32)
    hidden16 = gelu_tanh(hidden_pre).astype(low16)
    result = resid + jnp.dot(hidden16, mat_down, preferred_element_type=f32) + bias_down.astype(f32)
    out = result.astype(low16)
    again = (
        lax.all_gather(attn_gain, ("fsdp", "rep"), axis=0, tiled=True),
        lax.all_gather(attn_shift, ("fsdp", "rep"), axis=0, tiled=True),
        lax.all_gather(qkv_weight, ("fsdp", "rep"), axis=0, tiled=True),
        lax.all_gather(query_bias, ("fsdp", "rep"), axis=0, tiled=True),
        lax.all_gather(value_bias, ("fsdp", "rep"), axis=0, tiled=True),
        lax.all_gather(out_weight, ("fsdp", "rep"), axis=0, tiled=True),
        lax.all_gather(out_bias, ("fsdp", "rep"), axis=0, tiled=True),
        lax.all_gather(mlp_gain, ("fsdp", "rep"), axis=0, tiled=True),
        lax.all_gather(mlp_shift, ("fsdp", "rep"), axis=0, tiled=True),
        lax.all_gather(up_weight, ("fsdp", "rep"), axis=0, tiled=True),
        lax.all_gather(up_bias, ("fsdp", "rep"), axis=0, tiled=True),
        lax.all_gather(down_weight, ("fsdp", "rep"), axis=0, tiled=True),
        lax.all_gather(down_bias, ("fsdp", "rep"), axis=0, tiled=True),
    )
    (
        gain_attn,
        shift_attn,
        mat_qkv,
        bias_query,
        bias_value,
        mat_out,
        bias_out,
        gain_mlp,
        shift_mlp,
        mat_up,
        bias_up,
        mat_down,
        bias_down,
    ) = again
    grad_out = cotangent.astype(f32)
    grad_down_weight = jnp.einsum("nf,nd->fd", hidden16, cotangent, preferred_element_type=f32)
    grad_down_bias = jnp.sum(grad_out, axis=0)
    grad_hidden = jnp.einsum("nd,fd->nf", cotangent, mat_down, preferred_element_type=f32)
    unused, gelu_pull = jax.vjp(gelu_tanh, hidden_pre)
    grad_pre16 = gelu_pull(grad_hidden)[0].astype(low16)
    grad_up_weight = jnp.einsum("nd,nf->df", normed_mlp16, grad_pre16, preferred_element_type=f32)
    grad_up_bias = jnp.sum(grad_pre16.astype(f32), axis=0)
    grad_normed_mlp = jnp.einsum("nf,df->nd", grad_pre16, mat_up, preferred_element_type=f32)
    unused, second_pull = jax.vjp(norm_rows, resid, gain_mlp.astype(f32), shift_mlp.astype(f32))
    grad_resid_part, grad_mlp_gain, grad_mlp_shift = second_pull(grad_normed_mlp)
    grad_resid = grad_out + grad_resid_part
    grad_branch16 = grad_resid.astype(low16)
    grad_out_weight = jnp.einsum("ne,nd->ed", attended16, grad_branch16, preferred_element_type=f32)
    grad_out_bias = jnp.sum(grad_branch16.astype(f32), axis=0)
    grad_attended16 = jnp.einsum(
        "nd,ed->ne", grad_branch16, mat_out, preferred_element_type=f32
    ).astype(low16)
    grad_heads = grad_attended16.reshape(seq_count, LEN, HEADS, head_dim)
    grad_parts = []
    for number in range(block_count):
        first_seq = number * seq_span
        current = heads_view[first_seq : first_seq + seq_span]
        allowed = block_mask(segments[first_seq : first_seq + seq_span])
        scores = masked_scores(current[:, :, 0], current[:, :, 1], allowed, score_scale)
        probs = jnp.exp(scores - lse_parts[number])
        probs_low = probs.astype(low16)
        grad_block = grad_heads[first_seq : first_seq + seq_span]
        grad_probs = jnp.einsum(
            "sqhd,skhd->shqk", grad_block, current[:, :, 2], preferred_element_type=f32
        )
        grad_value = jnp.einsum(
            "shqk,sqhd->skhd", probs_low, grad_block, preferred_element_type=f32
        )
        inner = jnp.sum(probs * grad_probs, axis=-1, keepdims=True)
        grad_scores = (probs * (grad_probs - inner)).astype(low16)
        grad_query = (
            jnp.einsum("shqk,skhd->sqhd", grad_scores, current[:, :, 1], preferred_element_type=f32)
            * score_scale
        )
        grad_key = (
            jnp.einsum("shqk,sqhd->skhd", grad_scores, current[:, :, 0], preferred_element_type=f32)
            * score_scale
        )
        stacked = jnp.stack([grad_query, grad_key, grad_value], axis=2).reshape(
            seq_span * LEN, 3 * D
        )
        grad_parts.append(stacked.astype(low16))
    grad_qkv16 = jnp.concatenate(grad_parts, axis=0)
    grad_qkv_weight = jnp.einsum("nd,nc->dc", normed16, grad_qkv16, preferred_element_type=f32)
    bias_sums = jnp.sum(grad_qkv16.astype(f32), axis=0)
    grad_query_bias = bias_sums[:D]
    grad_value_bias = bias_sums[2 * D :]
    grad_normed = jnp.einsum("nc,dc->nd", grad_qkv16, mat_qkv, preferred_element_type=f32)
    unused, first_pull = jax.vjp(norm_rows, rows_in, gain_attn.astype(f32), shift_attn.astype(f32))
    grad_rows_part, grad_attn_gain, grad_attn_shift = first_pull(grad_normed)
    grad_tokens = grad_resid + grad_rows_part
    shares = (
        lax.psum_scatter(grad_attn_gain, ("fsdp", "rep"), scatter_dimension=0, tiled=True),
        lax.psum_scatter(grad_attn_shift, ("fsdp", "rep"), scatter_dimension=0, tiled=True),
        lax.psum_scatter(grad_qkv_weight, ("fsdp", "rep"), scatter_dimension=0, tiled=True),
        lax.psum_scatter(grad_query_bias, ("fsdp", "rep"), scatter_dimension=0, tiled=True),
        lax.psum_scatter(grad_value_bias, ("fsdp", "rep"), scatter_dimension=0, tiled=True),
        lax.psum_scatter(grad_out_weight, ("fsdp", "rep"), scatter_dimension=0, tiled=True),
        lax.psum_scatter(grad_out_bias, ("fsdp", "rep"), scatter_dimension=0, tiled=True),
        lax.psum_scatter(grad_mlp_gain, ("fsdp", "rep"), scatter_dimension=0, tiled=True),
        lax.psum_scatter(grad_mlp_shift, ("fsdp", "rep"), scatter_dimension=0, tiled=True),
        lax.psum_scatter(grad_up_weight, ("fsdp", "rep"), scatter_dimension=0, tiled=True),
        lax.psum_scatter(grad_up_bias, ("fsdp", "rep"), scatter_dimension=0, tiled=True),
        lax.psum_scatter(grad_down_weight, ("fsdp", "rep"), scatter_dimension=0, tiled=True),
        lax.psum_scatter(grad_down_bias, ("fsdp", "rep"), scatter_dimension=0, tiled=True),
    )
    shares = tuple(shares)
    return (out, grad_tokens) + shares


def solution(mesh):
    in_specs = (
        P(("fsdp", "rep"), None),
        P(("fsdp", "rep"), None),
        P(("fsdp", "rep"), None),
        P(("fsdp", "rep")),
        P(("fsdp", "rep")),
        P(("fsdp", "rep"), None),
        P(("fsdp", "rep")),
        P(("fsdp", "rep")),
        P(("fsdp", "rep"), None),
        P(("fsdp", "rep")),
        P(("fsdp", "rep")),
        P(("fsdp", "rep")),
        P(("fsdp", "rep"), None),
        P(("fsdp", "rep")),
        P(("fsdp", "rep"), None),
        P(("fsdp", "rep")),
    )
    out_specs = (
        P(("fsdp", "rep"), None),
        P(("fsdp", "rep"), None),
        P(("fsdp", "rep")),
        P(("fsdp", "rep")),
        P(("fsdp", "rep"), None),
        P(("fsdp", "rep")),
        P(("fsdp", "rep")),
        P(("fsdp", "rep"), None),
        P(("fsdp", "rep")),
        P(("fsdp", "rep")),
        P(("fsdp", "rep")),
        P(("fsdp", "rep"), None),
        P(("fsdp", "rep")),
        P(("fsdp", "rep"), None),
        P(("fsdp", "rep")),
    )
    return jax.shard_map(local, mesh=mesh, in_specs=in_specs, out_specs=out_specs, check_vma=False)
```

profile of v0, /device:TPU:0, one launch (start us, length us, event | category | flops | bytes accessed | tf_op | source)
XLA Modules:
  0.0 900.2 jit_solution(495881154036471823)
XLA Ops:
  17.6 42.7 %all-reduce.19 = (bf16[768]{0:T(1024)(128)(2,1)S(1)}, bf16[768]{0:T(1024)(128)(2,1)S(1)}, bf16[768]{0:T(1024)(128)(2,1)S(1)}, bf16[768]{0:T(1024)(128)(2,1)S(1)}...) all-reduce(bf16[768]{0:T(1024)(128)(2,1)S(1)} %dynamic-update-slice, ...), channel_id=1, replica_groups=mesh['fsdp'=16,'rep'=2] {'fsdp','rep'}, use_global_device_ids=true, to_apply=%add.3 | all-reduce | flops 9216 | bytes 36864
  60.3 2.8 copy.115
  64.9 4.3 copy.135
  70.2 3.9 all-gather.5.cloned.1.call-done
  74.1 8.4 add_convert_fusion
  82.5 3.2 fusion.85
  85.7 4.3 copy.128
  90.0 6.0 slice.112
  96.0 3.1 fusion.87
  105.0 4.3 copy.122
  109.3 6.0 slice.106
  115.3 3.0 fusion.88
  125.0 4.3 copy.116
  129.3 6.2 slice.100
  135.5 2.9 fusion.89
  147.0 4.4 fusion.95
  151.5 2.1 copy-done.6
  154.2 41.4 %all-gather.9.cloned.1.call-done = bf16[768,3072]{1,0:T(8,128)(2,1)} async-done(((bf16[24,3072]{1,0:T(8,128)(2,1)}), bf16[768,3072]{1,0:T(8,128)(2,1)}) %all-gather.9.cloned.1.call-update) | async-done | bytes 4718608 | tf_op jit(solution)/shard_map/all_gather | solution.py:70
  195.7 21.5 %multiply_convert_fusion = (bf16[1536,3072]{1,0:T(8,128)(2,1)}, f32[1536,3072]{1,0:T(8,128)}) fusion(f32[3072]{0:T(1024)S(1)} %convert_element_type.122, bf16[768,3072]{1,0:T(8,128)(2,1)} %all-gather.9.cloned.1.call-done, f32[1536,768]{0,1:T(8,128)} %copy-done.6, f32[768]{0:T(1024)S(1)} %convert_element_type.120, f32[768]{0:T(1024)S(1)} %convert_element_type.119, ...), kind=kOutput, calls=%fused_computation.11 | convolution fusion | flops 7300841472 | bytes 37779456 | tf_op jit(solution)/shard_map/dot_general | solution.py:124
  217.1 43.8 %all-gather.11.cloned.1.call-done = bf16[3072,768]{1,0:T(8,128)(2,1)} async-done(((bf16[96,768]{1,0:T(8,128)(2,1)}), bf16[3072,768]{1,0:T(8,128)(2,1)}) %all-gather.11.cloned.1.call-update) | async-done | bytes 4718608 | tf_op jit(solution)/shard_map/all_gather | solution.py:72
  260.9 25.2 %convert_reduce_fusion = (f32[3072]{0:T(1024)}, bf16[1536,3072]{1,0:T(8,128)(2,1)S(1)}) fusion(bf16[1536,768]{1,0:T(8,128)(2,1)S(1)} %copy-done.37, bf16[3072,768]{1,0:T(8,128)(2,1)} %all-gather.11.cloned.1.call-done, f32[1536,3072]{1,0:T(8,128)} %get-tuple-element.120, f32[3072]{0:T(1024)S(1)} %convert_element_type.122), kind=kOutput, calls=%fused_computation.10 | convolution fusion | flops 7375156224 | bytes 35414016 | tf_op jit(solution)/shard_map/nd,fd->nf/dot_general | solution.py:161
  286.2 9.9 %fusion.97 = (f32[768]{0:T(1024)}, f32[1536,768]{1,0:T(8,128)}) fusion(bf16[1536,3072]{1,0:T(8,128)(2,1)S(1)} %get-tuple-element.132, bf16[768,3072]{1,0:T(8,128)(2,1)S(1)} %copy-done.53), kind=kOutput, calls=%fused_computation.160 | convolution fusion | flops 7248935936 | bytes 18877440 | tf_op jit(solution)/shard_map/nf,df->nd/dot_general | solution.py:166
  296.1 6.1 copy.136
  302.2 5.2 multiply_reduce_fusion.3
  312.4 2.1 convolution_convert_fusion
  317.0 2.4 slice.122
  319.4 4.8 multiply_reduce_fusion
  325.9 2.8 fusion.64
  328.7 1.9 fusion.65
  330.6 2.0 fusion.48
  334.2 4.8 multiply_reduce_fusion.1
  339.0 4.6 multiply_convert_fusion.2
  343.6 2.7 fusion.62
  346.3 2.0 fusion.63
  348.3 1.9 fusion.51
  350.2 2.3 copy.137
  352.5 2.6 slice.118
  355.2 4.8 multiply_reduce_fusion.2
  361.7 2.7 fusion.60
  364.4 1.9 fusion.61
  366.3 1.9 fusion.54
  368.2 5.3 fusion.98
  373.8 2.5 copy.157
  376.3 1.8 copy.190
  378.4 2.6 copy.150
  381.1 1.8 copy.189
  383.2 2.5 copy.143
  386.5 2.0 constant_dynamic-update-slice_fusion.4
  388.8 2.9 copy-done.11
  391.7 8.3 fusion.78
  400.0 13.9 %fusion.81 = f32[768,3072]{1,0:T(8,128)} fusion(bf16[1536,3072]{1,0:T(8,128)(2,1)} %copy-done.55, f32[1536,768]{0,1:T(8,128)} %copy-done.6, f32[768]{0:T(1024)S(1)} %convert_element_type.120, f32[768]{0:T(1024)S(1)} %convert_element_type.119, f32[1536]{0:T(1024)S(1)} %fusion.77, f32[1536]{0:T(1024)S(1)} %broadcast_multiply_fusion), kind=kOutput, calls=%fused_computation.145 | convolution fusion | flops 7253655552 | bytes 23611392 | tf_op jit(solution)/shard_map/nd,nf->df/dot_general | solution.py:164
  413.9 13.4 %fusion.99 = f32[3072,768]{1,0:T(8,128)} fusion(bf16[1536,3072]{1,0:T(8,128)(2,1)} %get-tuple-element.119, bf16[1536,768]{1,0:T(8,128)(2,1)} %param.18), kind=kOutput, calls=%fused_computation.162 | convolution fusion | flops 7247757312 | bytes 21233664 | tf_op jit(solution)/shard_map/nf,nd->fd/dot_general | solution.py:159
  428.0 10.4 %fusion.96 = (f32[768]{0:T(1024)S(1)}, f32[1536,768]{1,0:T(8,128)}) fusion(bf16[1536,2304]{0,1:T(8,128)(2,1)} %copy-done.11, bf16[768,2304]{1,0:T(8,128)(2,1)} %all-gather.5.cloned.1.call-done), kind=kOutput, calls=%fused_computation.159 | convolution fusion | flops 5436996608 | bytes 15338496 | tf_op jit(solution)/shard_map/nc,dc->nd/dot_general | solution.py:211
  438.4 6.1 copy.158
  444.5 4.2 convert_reduce_fusion.1
  450.0 2.3 fusion.20
  452.3 4.3 convert_reduce_fusion.3
  456.6 40.7 %all-reduce.18 = (f32[768]{0:T(1024)S(1)}, f32[768]{0:T(1024)S(1)}, f32[768]{0:T(1024)S(1)}, f32[768]{0:T(1024)S(1)}, f32[768]{0:T(1024)S(1)}, /*index=5*/f32[76...) all-reduce(f32[768]{0:T(1024)S(1)} %get-tuple-element.62, ...), channel_id=2, replica_groups=mesh['fsdp'=16,'rep'=2] {'fsdp','rep'}, use_global_device_ids=true, to_apply=%region_18.19.clone | all-reduce | flops 9216 | bytes 73728
  502.0 6.2 copy.162
  508.2 12.7 %add_convert_fusion.1 = bf16[1536,768]{0,1:T(8,128)(2,1)S(1)} fusion(f32[1536,768]{0,1:T(8,128)} %copy-done.6, bf16[1536,3072]{1,0:T(8,128)(2,1)} %get-tuple-element.119, bf16[3072,768]{1,0:T(8,128)(2,1)} %all-gather.11.cloned.1.call-done, f32[768]{0:T(1024)S(1)} %convert_element_type.124), kind=kOutput, calls=%fused_computation.60 | convolution fusion | flops 7251296256 | bytes 21236736 | tf_op jit(solution)/shard_map/dot_general | solution.py:126
  520.9 2.4 copy.161
  523.9 85.6 %reduce-scatter.5.cloned.1.call-done = f32[24,2304]{1,0:T(8,128)} async-done(((f32[768,2304]{1,0:T(8,128)}), f32[24,2304]{1,0:T(8,128)}) %reduce-scatter.5.cloned.1.call-update) | async-done | bytes 221200 | tf_op jit(solution)/shard_map/reduce_scatter | solution.py:218
  609.5 141.3 %reduce-scatter.9.cloned.1.call-done = f32[24,3072]{1,0:T(8,128)} async-done(((f32[768,3072]{1,0:T(8,128)}), f32[24,3072]{1,0:T(8,128)}) %reduce-scatter.9.cloned.1.call-update) | async-done | bytes 294928 | tf_op jit(solution)/shard_map/reduce_scatter | solution.py:225
  750.7 142.2 %reduce-scatter.11.cloned.1.call-done = f32[96,768]{1,0:T(8,128)} async-done(((f32[3072,768]{1,0:T(8,128)}), f32[96,768]{1,0:T(8,128)}) %reduce-scatter.11.cloned.1.call-update) | async-done | bytes 294928 | tf_op jit(solution)/shard_map/reduce_scatter | solution.py:227
  (242 shorter events, 56.0 us)
Async XLA Ops:
  7.2 66.9 %all-gather.5.cloned.1.call-start = ((), (), s32[]{:S(2)}) async-start(), calls=%async_computation.4 | async-start | bytes 3649536 | tf_op jit(solution)/shard_map/all_gather | solution.py:63
  7.9 139.1 %all-gather.7.cloned.1.call-start = ((), (), s32[]{:S(2)}) async-start(), calls=%async_computation.5 | async-start | bytes 1216512 | tf_op jit(solution)/shard_map/all_gather | solution.py:66
  8.7 187.0 %all-gather.9.cloned.1.call-start = ((), (), s32[]{:S(2)}) async-start(), calls=%async_computation.6 | async-start | bytes 4866048 | tf_op jit(solution)/shard_map/all_gather | solution.py:70
  9.4 251.5 %all-gather.11.cloned.1.call-start = ((), (), s32[]{:S(2)}) async-start(), calls=%async_computation.7 | async-start | bytes 4866048 | tf_op jit(solution)/shard_map/all_gather | solution.py:72
  10.0 513.9 %reduce-scatter.7.cloned.1.call-start = ((), (), s32[]{:S(2)}) async-start(), calls=%async_computation.9 | async-start | bytes 2433024 | tf_op jit(solution)/shard_map/reduce_scatter | solution.py:221
  60.3 13.8 %copy-start.45 = (f32[768]{0:T(1024)}, f32[768]{0:T(1024)S(1)}, u32[]{:S(2)}) copy-start(f32[768]{0:T(1024)S(1)} %convert_element_type.109) | copy-start | bytes 9220
  60.3 13.8 %copy-start.49 = (f32[768]{0:T(1024)}, f32[768]{0:T(1024)S(1)}, u32[]{:S(2)}) copy-start(f32[768]{0:T(1024)S(1)} %convert_element_type.110) | copy-start | bytes 9220
  60.3 4.5 copy-start.48
  63.2 83.8 %copy-start.3 = (bf16[1536,768]{0,1:T(8,128)(2,1)}, bf16[1536,768]{0,1:T(8,128)(2,1)S(1)}, u32[]{:S(2)}) copy-start(bf16[1536,768]{0,1:T(8,128)(2,1)S(1)} %copy.115) | copy-start | bytes 7077892
  63.6 18.9 %copy-start.38 = (f32[1536]{0:T(1024)}, f32[1536]{0:T(1024)S(1)}, u32[]{:S(2)}) copy-start(f32[1536]{0:T(1024)S(1)} %broadcast_multiply_fusion.1) | copy-start | bytes 18436
  64.8 17.6 %copy-start.43 = (f32[1536]{0:T(1024)}, f32[1536]{0:T(1024)S(1)}, u32[]{:S(2)}) copy-start(f32[1536]{0:T(1024)S(1)} %fusion.76) | copy-start | bytes 18436
  99.1 2.2 copy-start.19
  99.1 3.3 copy-start.22
  101.3 2.7 copy-start
  115.3 3.9 copy-start.40
  118.3 2.2 copy-start.20
  118.3 3.3 copy-start.23
  120.5 2.6 copy-start.1
  138.4 2.2 copy-start.21
  138.4 3.2 copy-start.24
  140.6 2.6 copy-start.2
  151.5 2.1 copy-start.6
  154.2 106.7 %copy-start.37 = (bf16[1536,768]{1,0:T(8,128)(2,1)S(1)}, bf16[1536,768]{1,0:T(8,128)(2,1)}, u32[]{:S(2)}) copy-start(bf16[1536,768]{1,0:T(8,128)(2,1)} %param.18) | copy-start | bytes 7077892
  260.9 25.2 %copy-start.53 = (bf16[768,3072]{1,0:T(8,128)(2,1)S(1)}, bf16[768,3072]{1,0:T(8,128)(2,1)}, u32[]{:S(2)}) copy-start(bf16[768,3072]{1,0:T(8,128)(2,1)} %all-gather.9.cloned.1.call-done) | copy-start | bytes 14155780
  286.2 9.9 %copy-start.55 = (bf16[1536,3072]{1,0:T(8,128)(2,1)}, bf16[1536,3072]{1,0:T(8,128)(2,1)S(1)}, u32[]{:S(2)}) copy-start(bf16[1536,3072]{1,0:T(8,128)(2,1)S(1)} %get-tuple-element.132) | copy-start | bytes 28311556
  296.1 11.3 %slice-start.6 = ((s8[4718592]{0:T(1024)(128)(4,1)}), s8[524288]{0:T(1024)(128)(4,1)S(1)}, s32[]{:S(2)}) async-start(s8[4718592]{0:T(1024)(128)(4,1)} %bitcast.170), calls=%async_computation.18 | async-start | bytes 1048576
  302.2 5.2 slice-start.7
  302.2 6.4 copy-start.8
  310.2 2.2 copy-start.54
  311.9 2.6 copy-start.35
  314.5 9.8 %slice-start = ((s8[6291456]{0:T(1024)(128)(4,1)}), s8[2097152]{0:T(1024)(128)(4,1)S(1)}, s32[]{:S(2)}) async-start(s8[6291456]{0:T(1024)(128)(4,1)} %bitcast.164), calls=%async_computation.12 | async-start | bytes 4194304
  319.4 4.8 slice-start.1
  325.9 2.8 copy-start.14
  334.2 14.1 %slice-start.2 = ((s8[6291456]{0:T(1024)(128)(4,1)}), s8[4194304]{0:T(1024)(128)(4,1)S(1)}, s32[]{:S(2)}) async-start(s8[6291456]{0:T(1024)(128)(4,1)} %bitcast.166), calls=%async_computation.14 | async-start | bytes 8388608
  339.0 9.3 %slice-start.3 = ((s8[6291456]{0:T(1024)(128)(4,1)}), s8[2097152]{0:T(1024)(128)(4,1)S(1)}, s32[]{:S(2)}) async-start(s8[6291456]{0:T(1024)(128)(4,1)} %bitcast.166), calls=%async_computation.15 | async-start | bytes 4194304
  343.6 2.8 copy-start.16
  348.3 11.7 %slice-start.4 = ((s8[6291456]{0:T(1024)(128)(4,1)}), s8[2097152]{0:T(1024)(128)(4,1)S(1)}, s32[]{:S(2)}) async-start(s8[6291456]{0:T(1024)(128)(4,1)} %bitcast.168), calls=%async_computation.16 | async-start | bytes 4194304
  355.2 4.8 slice-start.5
  361.7 2.7 copy-start.18
  368.2 5.3 copy-start.25
  368.2 5.3 copy-start.26
  368.2 5.3 copy-start.32
  373.8 4.3 copy-start.27
  373.8 4.3 copy-start.28
  373.8 4.3 copy-start.33
  378.4 4.5 copy-start.29
  378.4 4.5 copy-start.30
  378.4 4.5 copy-start.34
  386.2 223.3 %reduce-scatter.5.cloned.1.call-start = ((), (), s32[]{:S(2)}) async-start(), calls=%async_computation.8 | async-start | bytes 7299072 | tf_op jit(solution)/shard_map/reduce_scatter | solution.py:218
  386.2 2.4 copy-start.12
  386.4 5.2 copy-start.4
  386.4 5.2 copy-start.39
  386.4 5.2 copy-start.44
  386.4 5.2 copy-start.46
  386.4 5.2 copy-start.50
  388.8 2.9 copy-start.11
  399.9 350.8 %reduce-scatter.9.cloned.1.call-start = ((), (), s32[]{:S(2)}) async-start(), calls=%async_computation.10 | async-start | bytes 9732096 | tf_op jit(solution)/shard_map/reduce_scatter | solution.py:225
  413.9 479.1 %reduce-scatter.11.cloned.1.call-start = ((), (), s32[]{:S(2)}) async-start(), calls=%async_computation.11 | async-start | bytes 9732096 | tf_op jit(solution)/shard_map/reduce_scatter | solution.py:227
  444.5 4.4 copy-start.5
  444.5 7.7 slice-start.8
  449.0 3.3 slice-start.9
  449.9 2.3 copy-start.10
  452.3 4.4 copy-start.47
  452.3 4.4 copy-start.51
  (10 other events, 12.8 us)
Sparse Core Ops, SparseCore 0:
  10.9 63.0 all-gather.4
  77.0 53.1 all-gather.6
  133.0 62.5 all-gather.8
  198.4 62.4 all-gather.10
  386.3 97.9 reduce-scatter.6
  491.3 118.0 reduce-scatter.4
  616.0 134.7 reduce-scatter.8
  758.2 134.6 reduce-scatter.10
where the time goes:
time: 910 us; the launch traced here: 900 us
  waiting for transfers between devices  461 us (51%)
  matrix products  177 us (19%)
  local copies, waits for them, and re-layouts  130 us (14%)
  blocking collectives  83.3 us (9%)
  other arithmetic  33.2 us (4%)
  between operations  15.6 us (2%)
    reduce_scatter x1, waiting for transfers between devices, local(): lax.psum_scatter(grad_down_weight, ('fsdp', 'rep'), scatter_dimension=0,...  142 us
    reduce_scatter x1, waiting for transfers between devices, local(): lax.psum_scatter(grad_up_weight, ('fsdp', 'rep'), scatter_dimension=0, ti...  141 us
    reduce_scatter x1, waiting for transfers between devices, local(): lax.psum_scatter(grad_qkv_weight, ('fsdp', 'rep'), scatter_dimension=0, t...  85.6 us
    unnamed x2, blocking collectives  83.3 us
    unnamed x173, local copies, waits for them, and re-layouts  51.6 us
    all_gather x1, waiting for transfers between devices, local(): lax.all_gather(down_weight, ('fsdp', 'rep'), axis=0, tiled=True)  43.8 us
    all_gather x1, waiting for transfers between devices, local(): lax.all_gather(up_weight, ('fsdp', 'rep'), axis=0, tiled=True)  41.4 us
    slice x7, local copies, waits for them, and re-layouts, local(): current = heads_view[first_seq:first_seq + seq_span]  34.4 us
  transfers between devices with their start and end apart: 8, of which 6 were waited for; matrix products, arithmetic and copies ran while one was open for 23% of the time, Pallas kernels for 0%

commit v1 on v0

--- a/solution.py
+++ b/solution.py
@@ -1,8 +1,11 @@
+import functools
 import math
 
 import jax
 import jax.numpy as jnp
 from jax import lax
+from jax.experimental import pallas as pl
+from jax.experimental.pallas import tpu as pltpu
 from jax.sharding import PartitionSpec as P
 
 D = 768
@@ -11,6 +14,299 @@
 
 
 EPSILON = 1e-05
+CHUNK = 32
+AXES = ("fsdp", "rep")
+PLACES = ("zh", "zl", "x", "c", "y")
+MESH = pl.DeviceIdType.MESH
+
+
+def places_and_partners():
+    f = lax.axis_index("fsdp")
+    r = lax.axis_index("rep")
+    where = {"zh": f // 8, "zl": (f // 4) % 2, "x": (f // 2) % 2, "c": f % 2, "y": r}
+    partner = {
+        "zh": (f + 8 - 16 * where["zh"], r),
+        "zl": (f + 4 - 8 * where["zl"], r),
+        "x": (f + 2 - 4 * where["x"], r),
+        "c": (f + 1 - 2 * where["c"], r),
+        "y": (f, 1 - r),
+    }
+    return where, partner
+
+
+def greet(partner):
+    barrier = pltpu.get_barrier_semaphore()
+    for name in PLACES:
+        pl.semaphore_signal(barrier, inc=1, device_id=partner[name], device_id_type=MESH)
+    pl.semaphore_wait(barrier, len(PLACES))
+
+
+def gather_kernel(chunk, block_ref, all_ref, send_sem, recv_sem, own_sem):
+    where, partner = places_and_partners()
+    chunks = block_ref.shape[0] // chunk
+    own = pltpu.make_async_copy(
+        block_ref, all_ref.at[tuple(where[name] for name in PLACES)], own_sem
+    )
+    own.start()
+    greet(partner)
+    orders = (("zh", "zl", "x", "y", "c"), ("zh", "zl", "y", "x", "c"))
+    copies = {}
+
+    def begin(number, step):
+        order = orders[number % 2]
+        rows = pl.ds(number * chunk, chunk)
+        index = tuple(
+            slice(None) if name in order[:step] else where[name] for name in PLACES
+        ) + (rows,)
+        source = block_ref.at[rows] if step == 0 else all_ref.at[index]
+        copy = pltpu.make_async_remote_copy(
+            src_ref=source,
+            dst_ref=all_ref.at[index],
+            send_sem=send_sem.at[number, step],
+            recv_sem=recv_sem.at[number, step],
+            device_id=partner[order[step]],
+            device_id_type=MESH,
+        )
+        copy.start()
+        copies[number, step] = copy
+
+    pairs = chunks // 2
+    steps = len(PLACES)
+    for wave in range(pairs + steps):
+        for pair in range(pairs):
+            step = wave - pair
+            if not 0 <= step <= steps:
+                continue
+            for number in (2 * pair, 2 * pair + 1):
+                if step == 1 and number == 0:
+                    own.wait()
+                if step > 0:
+                    copies[number, step - 1].wait_recv()
+                if step < steps:
+                    begin(number, step)
+    for copy in copies.values():
+        copy.wait_send()
+
+
+def gather_all(block, chunk):
+    rows, width = block.shape
+    chunks = rows // chunk
+    return pl.pallas_call(
+        functools.partial(gather_kernel, chunk),
+        out_shape=jax.ShapeDtypeStruct((2,) * 5 + (rows, width), block.dtype),
+        in_specs=[pl.BlockSpec(memory_space=pl.ANY)],
+        out_specs=pl.BlockSpec(memory_space=pl.ANY),
+        scratch_shapes=[
+            pltpu.SemaphoreType.DMA((chunks, 5)),
+            pltpu.SemaphoreType.DMA((chunks, 5)),
+            pltpu.SemaphoreType.DMA,
+        ],
+        compiler_params=pltpu.CompilerParams(collective_id=0, has_side_effects=True),
+    )(block)
+
+
+def scatter_kernel(
+    chunk, parts_ref, sum_ref, held, got0, got1, got2, got3, got4, send_sem, recv_sem, own_sem
+):
+    where, partner = places_and_partners()
+    chunks = parts_ref.shape[5] // chunk
+    zh, zl, x, c, y = (where[name] for name in PLACES)
+    everything = slice(None)
+    f32 = jnp.float32
+
+    def rows_of(number):
+        return pl.ds(number * chunk, chunk)
+
+    own = []
+    for number in range(chunks):
+        rows = rows_of(number)
+        copy = pltpu.make_async_copy(
+            parts_ref.at[:, :, :, c, :, rows], held.at[:, :, :, :, rows], own_sem.at[number]
+        )
+        copy.start()
+        own.append(copy)
+    greet(partner)
+    copies = {}
+
+    def begin(number, step):
+        rows = rows_of(number)
+        x_first = number % 2 == 0
+        if step == 0:
+            name = "c"
+            source = parts_ref.at[:, :, :, 1 - c, :, rows]
+            target = got0.at[:, :, :, :, rows]
+        elif step == 1:
+            name = "x" if x_first else "y"
+            source = held.at[:, :, 1 - x, :, rows] if x_first else held.at[:, :, :, 1 - y, rows]
+            target = got1.at[:, :, :, rows]
+        elif step == 2:
+            name = "y" if x_first else "x"
+            source = held.at[:, :, x, 1 - y, rows] if x_first else held.at[:, :, 1 - x, y, rows]
+            target = got2.at[:, :, rows]
+        elif step == 3:
+            name = "zl"
+            source = held.at[:, 1 - zl, x, y, rows]
+            target = got3.at[:, rows]
+        else:
+            name = "zh"
+            source = held.at[1 - zh, zl, x, y, rows]
+            target = got4.at[rows]
+        copy = pltpu.make_async_remote_copy(
+            src_ref=source,
+            dst_ref=target,
+            send_sem=send_sem.at[number, step],
+            recv_sem=recv_sem.at[number, step],
+            device_id=partner[name],
+            device_id_type=MESH,
+        )
+        copy.start()
+        copies[number, step] = copy
+
+    def add(number, step):
+        rows = rows_of(number)
+        x_first = number % 2 == 0
+        copies[number, step].wait_recv()
+        if step == 0:
+            own[number].wait()
+
+        def add_one(at, value):
+            held[at] = (held[at].astype(f32) + value.astype(f32)).astype(held.dtype)
+
+        if step == 4:
+            at = (zh, zl, x, y, rows)
+            sum_ref[rows] = held[at].astype(f32) + got4[rows].astype(f32)
+            return
+
+        def body(i, carry):
+            if step == 0:
+                four = (i // 8, (i // 4) % 2, (i // 2) % 2, i % 2)
+                add_one(four + (rows,), got0[four + (rows,)])
+            elif step == 1:
+                three = (i // 4, (i // 2) % 2, i % 2)
+                if x_first:
+                    at = three[:2] + (x, three[2], rows)
+                else:
+                    at = three + (y, rows)
+                add_one(at, got1[three + (rows,)])
+            elif step == 2:
+                two = (i // 2, i % 2)
+                add_one(two + (x, y, rows), got2[two + (rows,)])
+            else:
+                add_one((i, zl, x, y, rows), got3[i, rows])
+            return carry
+
+        lax.fori_loop(0, 16 >> step, body, 0)
+
+    for number in range(chunks):
+        begin(number, 0)
+    pairs = chunks // 2
+    for wave in range(1, pairs + 5):
+        for pair in range(pairs):
+            step = wave - pair
+            if not 1 <= step <= 5:
+                continue
+            for number in (2 * pair, 2 * pair + 1):
+                add(number, step - 1)
+                if step < 5:
+                    begin(number, step)
+    for copy in copies.values():
+        copy.wait_send()
+
+
+def scatter_sum(parts, chunk):
+    rows, width = parts.shape[5:]
+    chunks = rows // chunk
+    low = parts.dtype
+    return pl.pallas_call(
+        functools.partial(scatter_kernel, chunk),
+        out_shape=jax.ShapeDtypeStruct((rows, width), jnp.float32),
+        in_specs=[pl.BlockSpec(memory_space=pl.ANY)],
+        out_specs=pl.BlockSpec(memory_space=pltpu.VMEM),
+        scratch_shapes=[
+            pltpu.VMEM((2, 2, 2, 2, rows, width), low),
+            pltpu.VMEM((2, 2, 2, 2, rows, width), low),
+            pltpu.VMEM((2, 2, 2, rows, width), low),
+            pltpu.VMEM((2, 2, rows, width), low),
+            pltpu.VMEM((2, rows, width), low),
+            pltpu.VMEM((rows, width), low),
+            pltpu.SemaphoreType.DMA((chunks, 5)),
+            pltpu.SemaphoreType.DMA((chunks, 5)),
+            pltpu.SemaphoreType.DMA((chunks,)),
+        ],
+        compiler_params=pltpu.CompilerParams(
+            collective_id=1, has_side_effects=True, vmem_limit_bytes=40 * 1024 * 1024
+        ),
+    )(parts)
+
+
+def columns_to_rows(weight):
+    return [weight[:, at : at + D] for at in range(0, weight.shape[1], D)]
+
+
+def gather_params(params):
+    ag, ash, wq, bq, bv, wo, bo, mg, ms, wu, bu, wd, bd = params
+    count = D // wq.shape[0]
+    if wq.shape[0] % 8 or count != 32:
+        return tuple(lax.all_gather(p, AXES, axis=0, tiled=True) for p in params)
+    small = jnp.concatenate([ag, ash, bq, bv, bo, mg, ms, bd, bu])
+    small = jnp.pad(small, (0, D - small.shape[0]))[None]
+    pieces = columns_to_rows(wq) + [wo] + columns_to_rows(wu) + [wd, small]
+    used = sum(piece.shape[0] for piece in pieces)
+    rows = -(-used // (2 * CHUNK)) * 2 * CHUNK
+    block = jnp.pad(jnp.concatenate(pieces, axis=0), ((0, rows - used), (0, 0)))
+    whole = gather_all(block, CHUNK).reshape(count, rows, D)
+    n, m = wq.shape[0], wd.shape[0]
+    at = 0
+
+    def wide(parts):
+        nonlocal at
+        taken = [whole[:, at + n * i : at + n * (i + 1)].reshape(D, D) for i in range(parts)]
+        at += n * parts
+        return jnp.concatenate(taken, axis=1) if parts > 1 else taken[0]
+
+    mat_qkv, mat_out, mat_up = wide(3), wide(1), wide(wu.shape[1] // D)
+    mat_down = whole[:, at : at + m].reshape(count * m, D)
+    line = whole[:, at + m]
+    vectors = [line[:, n * i : n * (i + 1)].reshape(D) for i in range(8)]
+    up_line = line[:, 8 * n : 8 * n + bu.shape[0]].reshape(-1)
+    a, b, c, d, e, f, g, h = vectors
+    return (a, b, mat_qkv, c, d, mat_out, e, f, g, mat_up, up_line, mat_down, h)
+
+
+def scatter_grads(grads, n, m):
+    ag, ash, wq, bq, bv, wo, bo, mg, ms, wu, bu, wd, bd = grads
+    count = D // n
+    if n % 8 or count != 32:
+        return tuple(lax.psum_scatter(g, AXES, scatter_dimension=0, tiled=True) for g in grads)
+    low16 = jnp.bfloat16
+    small = jnp.concatenate(
+        [v.reshape(count, n) for v in (ag, ash, bq, bv, bo, mg, ms, bd)] + [bu.reshape(count, -1)],
+        axis=1,
+    )
+    small = jnp.pad(small, ((0, 0), (0, D - small.shape[1])))[:, None].astype(low16)
+    pieces = [
+        part.reshape(count, n, D)
+        for weight in (wq, wo, wu)
+        for part in columns_to_rows(weight.astype(low16))
+    ] + [wd.astype(low16).reshape(count, m, D), small]
+    used = sum(piece.shape[1] for piece in pieces)
+    rows = -(-used // (2 * CHUNK)) * 2 * CHUNK
+    parts = jnp.pad(jnp.concatenate(pieces, axis=1), ((0, 0), (0, rows - used), (0, 0)))
+    total = scatter_sum(parts.reshape((2,) * 5 + (rows, D)), CHUNK)
+    at = 0
+
+    def wide(parts):
+        nonlocal at
+        taken = [total[at + n * i : at + n * (i + 1)] for i in range(parts)]
+        at += n * parts
+        return jnp.concatenate(taken, axis=1) if parts > 1 else taken[0]
+
+    g_qkv, g_out, g_up = wide(3), wide(1), wide(wu.shape[1] // D)
+    g_down = total[at : at + m]
+    line = total[at + m]
+    a, b, c, d, e, f, g, h = [line[n * i : n * (i + 1)] for i in range(8)]
+    up_line = line[8 * n : 8 * n + bu.shape[0] // count]
+    return (a, b, g_qkv, c, d, g_out, e, f, g, g_up, up_line, g_down, h)
 
 
 def norm_rows(values, gain, shift):
@@ -57,20 +353,9 @@
     down_weight,
     down_bias,
 ):
-    gathered = (
-        lax.all_gather(attn_gain, ("fsdp", "rep"), axis=0, tiled=True),
-        lax.all_gather(attn_shift, ("fsdp", "rep"), axis=0, tiled=True),
-        lax.all_gather(qkv_weight, ("fsdp", "rep"), axis=0, tiled=True),
-        lax.all_gather(query_bias, ("fsdp", "rep"), axis=0, tiled=True),
-        lax.all_gather(value_bias, ("fsdp", "rep"), axis=0, tiled=True),
-        lax.all_gather(out_weight, ("fsdp", "rep"), axis=0, tiled=True),
-        lax.all_gather(out_bias, ("fsdp", "rep"), axis=0, tiled=True),
-        lax.all_gather(mlp_gain, ("fsdp", "rep"), axis=0, tiled=True),
-        lax.all_gather(mlp_shift, ("fsdp", "rep"), axis=0, tiled=True),
-        lax.all_gather(up_weight, ("fsdp", "rep"), axis=0, tiled=True),
-        lax.all_gather(up_bias, ("fsdp", "rep"), axis=0, tiled=True),
-        lax.all_gather(down_weight, ("fsdp", "rep"), axis=0, tiled=True),
-        lax.all_gather(down_bias, ("fsdp", "rep"), axis=0, tiled=True),
+    gathered = gather_params(
+        (attn_gain, attn_shift, qkv_weight, query_bias, value_bias, out_weight, out_bias,
+         mlp_gain, mlp_shift, up_weight, up_bias, down_weight, down_bias)
     )
     (
         gain_attn,
@@ -125,36 +410,6 @@
     hidden16 = gelu_tanh(hidden_pre).astype(low16)
     result = resid + jnp.dot(hidden16, mat_down, preferred_element_type=f32) + bias_down.astype(f32)
     out = result.astype(low16)
-    again = (
-        lax.all_gather(attn_gain, ("fsdp", "rep"), axis=0, tiled=True),
-        lax.all_gather(attn_shift, ("fsdp", "rep"), axis=0, tiled=True),
-        lax.all_gather(qkv_weight, ("fsdp", "rep"), axis=0, tiled=True),
-        lax.all_gather(query_bias, ("fsdp", "rep"), axis=0, tiled=True),
-        lax.all_gather(value_bias, ("fsdp", "rep"), axis=0, tiled=True),
-        lax.all_gather(out_weight, ("fsdp", "rep"), axis=0, tiled=True),
-        lax.all_gather(out_bias, ("fsdp", "rep"), axis=0, tiled=True),
-        lax.all_gather(mlp_gain, ("fsdp", "rep"), axis=0, tiled=True),
-        lax.all_gather(mlp_shift, ("fsdp", "rep"), axis=0, tiled=True),
-        lax.all_gather(up_weight, ("fsdp", "rep"), axis=0, tiled=True),
-        lax.all_gather(up_bias, ("fsdp", "rep"), axis=0, tiled=True),
-        lax.all_gather(down_weight, ("fsdp", "rep"), axis=0, tiled=True),
-        lax.all_gather(down_bias, ("fsdp", "rep"), axis=0, tiled=True),
-    )
-    (
-        gain_attn,
-        shift_attn,
-        mat_qkv,
-        bias_query,
-        bias_value,
-        mat_out,
-        bias_out,
-        gain_mlp,
-        shift_mlp,
-        mat_up,
-        bias_up,
-        mat_down,
-        bias_down,
-    ) = again
     grad_out = cotangent.astype(f32)
     grad_down_weight = jnp.einsum("nf,nd->fd", hidden16, cotangent, preferred_element_type=f32)
     grad_down_bias = jnp.sum(grad_out, axis=0)
@@ -212,22 +467,13 @@
     unused, first_pull = jax.vjp(norm_rows, rows_in, gain_attn.astype(f32), shift_attn.astype(f32))
     grad_rows_part, grad_attn_gain, grad_attn_shift = first_pull(grad_normed)
     grad_tokens = grad_resid + grad_rows_part
-    shares = (
-        lax.psum_scatter(grad_attn_gain, ("fsdp", "rep"), scatter_dimension=0, tiled=True),
-        lax.psum_scatter(grad_attn_shift, ("fsdp", "rep"), scatter_dimension=0, tiled=True),
-        lax.psum_scatter(grad_qkv_weight, ("fsdp", "rep"), scatter_dimension=0, tiled=True),
-        lax.psum_scatter(grad_query_bias, ("fsdp", "rep"), scatter_dimension=0, tiled=True),
-        lax.psum_scatter(grad_value_bias, ("fsdp", "rep"), scatter_dimension=0, tiled=True),
-        lax.psum_scatter(grad_out_weight, ("fsdp", "rep"), scatter_dimension=0, tiled=True),
-        lax.psum_scatter(grad_out_bias, ("fsdp", "rep"), scatter_dimension=0, tiled=True),
-        lax.psum_scatter(grad_mlp_gain, ("fsdp", "rep"), scatter_dimension=0, tiled=True),
-        lax.psum_scatter(grad_mlp_shift, ("fsdp", "rep"), scatter_dimension=0, tiled=True),
-        lax.psum_scatter(grad_up_weight, ("fsdp", "rep"), scatter_dimension=0, tiled=True),
-        lax.psum_scatter(grad_up_bias, ("fsdp", "rep"), scatter_dimension=0, tiled=True),
-        lax.psum_scatter(grad_down_weight, ("fsdp", "rep"), scatter_dimension=0, tiled=True),
-        lax.psum_scatter(grad_down_bias, ("fsdp", "rep"), scatter_dimension=0, tiled=True),
-    )
-    shares = tuple(shares)
+    shares = scatter_grads(
+        (grad_attn_gain, grad_attn_shift, grad_qkv_weight, grad_query_bias, grad_value_bias,
+         grad_out_weight, grad_out_bias, grad_mlp_gain, grad_mlp_shift, grad_up_weight,
+         grad_up_bias, grad_down_weight, grad_down_bias),
+        qkv_weight.shape[0],
+        down_weight.shape[0],
+    )
     return (out, grad_tokens) + shares
 
 

time: 910 us -> 592 us (0.65)
  waiting for transfers between devices: 461 us -> 0 us
  Pallas kernels: 0 us -> 187 us
  blocking collectives: 83.3 us -> 0 us
  local copies, waits for them, and re-layouts: 130 us -> 175 us
  other arithmetic: 33.2 us -> 47.3 us
  between operations: 15.6 us -> 2.18 us
    reduce_scatter x4 -> x0, waiting for transfers between devices: 369 us -> none  [the longest x1 142 us: local(): lax.psum_scatter(grad_down_weight, ('fsdp', 'rep'), scatter_dimension=0,...]
    pallas_call x0 -> x2, Pallas kernels: none -> 187 us  [the longest x1 98 us: gather_all(): pl.pallas_call(functools.partial(gather_kernel, chunk), out_shape=jax.Sha...]
    all_gather x4 -> x0, waiting for transfers between devices: 89.1 us -> none  [the longest x1 43.8 us: local(): lax.all_gather(down_weight, ('fsdp', 'rep'), axis=0, tiled=True)]
    unnamed x2 -> x0, blocking collectives: 83.3 us -> none
    slice x0 -> x9, local copies, waits for them, and re-layouts: none -> 18.7 us  [the longest x1 6.36 us: wide(): whole[:, at + n * i:at + n * (i + 1)].reshape(D, D)]
    slice x3, local copies, waits for them, and re-layouts: 8.93 us -> 21.6 us  [local(): current[:, :, 2]]
    unnamed x173 -> x203, local copies, waits for them, and re-layouts: 51.6 us -> 40.7 us
  transfers between devices with their start and end apart: 8 -> 0, of which waited for: 6 -> 0; matrix products, arithmetic and copies ran while one was open for 23% -> 0% of each run, Pallas kernels for 0% -> 0%
where the time goes in v1:
time: 592 us; the launch traced here: 586 us
  Pallas kernels  187 us (32%)
  local copies, waits for them, and re-layouts  175 us (30%)
  matrix products  175 us (30%)
  other arithmetic  47.3 us (8%)
    pallas_call x1, Pallas kernels, gather_all(): pl.pallas_call(functools.partial(gather_kernel, chunk), out_shape=jax.Sha...  98 us
    pallas_call x1, Pallas kernels, scatter_sum(): pl.pallas_call(functools.partial(scatter_kernel, chunk), out_shape=jax.Sh...  88.6 us
    unnamed x203, local copies, waits for them, and re-layouts  40.7 us
    slice x7, local copies, waits for them, and re-layouts, local(): current = heads_view[first_seq:first_seq + seq_span]  34.4 us
    dot_general x1, matrix products, local(): jnp.einsum('nd,fd->nf', cotangent, mat_down, preferred_element_type=f32)  25.8 us
    dot_general x1, matrix products, local(): jnp.dot(normed_mlp16, mat_up, preferred_element_type=f32)  22.5 us
    slice x3, local copies, waits for them, and re-layouts, local(): current[:, :, 2]  21.6 us
    dot_general x3, matrix products, local(): jnp.einsum('shqk,sqhd->skhd', probs_low, grad_block, preferred_element_ty...  14.3 us

profile of v1, /device:TPU:0, one launch (start us, length us, event | category | flops | bytes accessed | tf_op | source)
XLA Modules:
  0.0 586.2 jit_solution(11069530557832070954)
XLA Ops:
  0.6 6.1 %concatenate.35 = bf16[288]{0:T(512)(128)(2,1)S(1)} concatenate(bf16[24]{0:T(256)(128)(2,1)} %param.19, bf16[24]{0:T(256)(128)(2,1)} %param.20, bf16[24]{0:T(256)(128)(2,1)} %param.22, bf16[24]{0:T(256)(128)(2,1)} %param.23, bf16[24]{0:T(256)(128)(2,1)} %param.25, bf16[24]{0:T(256)(128)(2,1)} %param.26, bf16[24]{0:T(256)(128)(2,1)} %param.27, bf16[24]{0:T(256)(128)(2,1)} %param.31, ...), dimensions={0} | concatenate | bytes 1152 | tf_op jit(solution)/shard_map/concatenate | solution.py:251
  6.8 2.1 reduce.2
  18.6 2.8 copy.67
  22.6 4.3 copy.88
  26.9 98.0 %shard_map.271 = bf16[2,2,2,2,2,320,768]{6,5,4,3,2,1,0:T(8,128)(2,1)} custom-call(bf16[320,768]{1,0:T(8,128)(2,1)} %pad.18.block_ref), custom_call_target="tpu_custom_call" | custom-call | tf_op jit(solution)/shard_map/pallas_call | solution.py:94
  128.7 4.8 slice.424
  133.5 6.4 %fusion.96 = (bf16[32,24,768]{2,1,0:T(8,128)(2,1)}, bf16[32,24,768]{2,1,0:T(8,128)(2,1)}, bf16[32,24,768]{2,1,0:T(8,128)(2,1)}, bf16[32,24,768]{2,1,0:T(8,128)(2...) fusion(bf16[32,320,768]{2,1,0:T(8,128)(2,1)} %bitcast.225), kind=kLoop, calls=%fused_computation.206 | loop fusion | bytes 18874368 | tf_op jit(solution)/shard_map/slice | solution.py:263
  139.9 7.7 %add_convert_fusion = bf16[1536,2304]{1,0:T(8,128)(2,1)S(1)} fusion(f32[2304]{0:T(1024)S(1)} %pad_maximum_fusion.11, bf16[768,768]{1,0:T(8,128)(2,1)S(1)} %bitcast.256, bf16[768,768]{1,0:T(8,128)(2,1)S(1)} %bitcast.258, bf16[768,768]{1,0:T(8,128)(2,1)S(1)} %bitcast.260, bf16[1536,768]{0,1:T(8,128)(2,1)S(1)} %copy.67, f32[768]{0:T(1024)S(1)} %reshape.395, ...), kind=kOutput, calls=%fused_computation.16 | convolution fusion | flops 5460590592 | bytes 13003776 | tf_op jit(solution)/shard_map/dot_general | solution.py:387
  147.7 3.1 fusion.97
  150.8 4.3 copy.81
  155.1 6.0 %slice.335 = bf16[2,256,3,12,64]{1,0,4,3,2:T(2,128)(2,1)} reshape(bf16[512,2304]{0,1:T(8,128)(2,1)} %copy.81) | data formatting | bytes 4718592 | tf_op jit(solution)/shard_map/slice | solution.py:393
  161.1 4.2 fusion.101
  165.3 4.6 copy.75
  169.9 6.0 %slice.329 = bf16[2,256,3,12,64]{1,0,4,3,2:T(2,128)(2,1)} reshape(bf16[512,2304]{0,1:T(8,128)(2,1)} %copy.75) | data formatting | bytes 4718592 | tf_op jit(solution)/shard_map/slice | solution.py:393
  175.9 14.5 %fusion.102 = (bf16[2,256,1,12,64]{1,0,4,3,2:T(2,128)(2,1)}, bf16[2,256,1,12,64]{1,0,4,3,2:T(2,128)(2,1)}, bf16[2,256,1,12,64]{1,0,4,3,2:T(2,128)(2,1)}) fusion(bf16[2,256,3,12,64]{1,0,4,3,2:T(2,128)(2,1)} %slice.329), kind=kLoop, calls=%fused_computation.212 | loop fusion | bytes 4718592 | tf_op jit(solution)/shard_map/slice | solution.py:402
  190.4 4.3 copy.69
  194.7 6.0 %slice.323 = bf16[2,256,3,12,64]{1,0,4,3,2:T(2,128)(2,1)} reshape(bf16[512,2304]{0,1:T(8,128)(2,1)} %copy.69) | data formatting | bytes 4718592 | tf_op jit(solution)/shard_map/slice | solution.py:393
  200.8 2.9 fusion.103
  220.1 1.6 fusion.63
  223.0 2.5 fusion.110
  225.5 2.2 copy-done.6
  228.3 22.5 %multiply_convert_fusion = (bf16[1536,3072]{1,0:T(8,128)(2,1)}, f32[1536,3072]{1,0:T(8,128)}) fusion(f32[3072]{0:T(1024)S(1)} %reshape.401, bf16[768,768]{1,0:T(8,128)(2,1)} %bitcast.266, bf16[768,768]{1,0:T(8,128)(2,1)} %bitcast.268, bf16[768,768]{1,0:T(8,128)(2,1)} %bitcast.270, bf16[768,768]{1,0:T(8,128)(2,1)} %bitcast.264, f32[1536,768]{0,1:T(8,128)} %copy-done.6, ...), kind=kOutput, calls=%fused_computation.15 | convolution fusion | flops 7319715840 | bytes 37779456 | tf_op jit(solution)/shard_map/dot_general | solution.py:409
  250.8 25.8 %fusion.113 = (bf16[3072]{0:T(1024)(128)(2,1)S(1)}, bf16[1536,3072]{1,0:T(8,128)(2,1)}) fusion(bf16[3072,768]{1,0:T(8,128)(2,1)} %bitcast.248, bf16[1536,768]{1,0:T(8,128)(2,1)S(1)} %copy-done.9, f32[1536,3072]{1,0:T(8,128)} %get-tuple-element.136, f32[3072]{0:T(1024)S(1)} %reshape.401), kind=kOutput, calls=%fused_computation.223 | convolution fusion | flops 7370437632 | bytes 35407872 | tf_op jit(solution)/shard_map/nd,fd->nf/dot_general | solution.py:416
  276.6 12.8 %add_convert_fusion.1 = bf16[1536,768]{0,1:T(8,128)(2,1)} fusion(f32[1536,768]{0,1:T(8,128)S(1)} %bitcast.227, bf16[1536,3072]{1,0:T(8,128)(2,1)} %get-tuple-element.135, bf16[3072,768]{1,0:T(8,128)(2,1)} %bitcast.249, f32[768]{0:T(1024)S(1)} %copy-done.69), kind=kOutput, calls=%fused_computation.65 | convolution fusion | flops 7251296256 | bytes 21236736 | tf_op jit(solution)/shard_map/dot_general | solution.py:411
  289.4 13.4 %convolution_convert_fusion = bf16[3072,768]{1,0:T(8,128)(2,1)} fusion(bf16[1536,3072]{1,0:T(8,128)(2,1)} %get-tuple-element.135, bf16[1536,768]{1,0:T(8,128)(2,1)S(1)} %copy-done.9), kind=kOutput, calls=%fused_computation.49 | convolution fusion | flops 7250116608 | bytes 16515072 | tf_op jit(solution)/shard_map/nf,nd->fd/dot_general | solution.py:414
  302.8 4.4 copy.115
  307.9 13.4 %fusion.112 = (bf16[768]{0:T(1024)(128)(2,1)S(1)}, f32[1536,768]{1,0:T(8,128)}) fusion(bf16[1536,3072]{1,0:T(8,128)(2,1)} %get-tuple-element.142, bf16[768,768]{1,0:T(8,128)(2,1)S(1)} %bitcast.267, bf16[768,768]{1,0:T(8,128)(2,1)} %bitcast.269, bf16[768,768]{1,0:T(8,128)(2,1)} %bitcast.271, bf16[768,768]{1,0:T(8,128)(2,1)S(1)} %bitcast.265), kind=kOutput, calls=%fused_computation.222 | convolution fusion | flops 7267810304 | bytes 18875904 | tf_op jit(solution)/shard_map/nf,df->nd/dot_general | solution.py:421
  321.3 10.1 %convolution_convert_fusion.2 = bf16[768,3072]{1,0:T(8,128)(2,1)S(1)} fusion(bf16[1536,3072]{1,0:T(8,128)(2,1)} %get-tuple-element.142, f32[1536,768]{0,1:T(8,128)S(1)} %bitcast.229, f32[768]{0:T(1024)S(1)} %copy-done.68, f32[768]{0:T(1024)S(1)} %reshape.399, f32[1536]{0:T(1024)S(1)} %fusion.83, f32[1536]{0:T(1024)S(1)} %broadcast_multiply_fusion), kind=kOutput, calls=%fused_computation.51 | convolution fusion | flops 7256014848 | bytes 18892800 | tf_op jit(solution)/shard_map/nd,nf->df/dot_general | solution.py:419
  331.4 2.3 fusion.98
  334.4 6.5 %copy.89 = f32[1536,768]{0,1:T(8,128)} copy(f32[1536,768]{1,0:T(8,128)} %get-tuple-element.140) | data formatting | bytes 9437184 | tf_op jit(solution)/shard_map/nf,df->nd/dot_general | solution.py:421
  340.9 5.2 multiply_reduce_fusion.3
  347.3 3.4 fusion.95
  351.4 3.2 fusion.90
  354.6 3.0 convolution_convert_fusion.4
  358.4 3.7 convolution_convert_fusion.3
  363.5 2.2 slice.356
  365.7 4.7 fusion.52
  371.6 2.2 slice.354
  373.9 4.7 fusion.55
  379.7 2.4 slice.352
  382.2 4.8 fusion.58
  387.0 7.1 %multiply_reduce_fusion.2 = (f32[2,12,256]{2,1,0:T(8,128)S(1)}, f32[2,12,256,256]{2,3,1,0:T(8,128)}) fusion(f32[2,12,256,256]{2,3,1,0:T(8,128)} %copy-done.1, f32[2,12,256]{2,1,0:T(8,128)S(1)} %copy-done.51, bf16[2,256,1,12,64]{1,0,4,3,2:T(2,128)(2,1)S(1)} %copy-done.32, bf16[2,256,12,64]{1,0,3,2:T(2,128)(2,1)S(1)} %slice.352), kind=kOutput, calls=%fused_computation.33 | convolution fusion | flops 206039040 | bytes 14204928 | tf_op jit(solution)/shard_map/sqhd,skhd->shqk/dot_general | solution.py:441
  394.1 4.6 multiply_convert_fusion.3
  398.7 3.3 fusion.65
  403.5 1.7 multiply_reduce_fusion.1
  405.2 1.7 multiply_convert_fusion.2
  409.8 2.5 copy.103
  412.8 2.5 copy.96
  415.8 1.7 constant_dynamic-update-slice_fusion.15
  417.5 1.6 constant_dynamic-update-slice_fusion.14
  419.1 2.1 multiply_reduce_fusion
  421.2 1.7 multiply_convert_fusion.1
  426.4 2.5 copy.110
  429.4 1.6 constant_dynamic-update-slice_fusion.13
  431.7 9.5 %fusion.111 = (bf16[768]{0:T(1024)(128)(2,1)S(1)}, f32[1536,768]{1,0:T(8,128)}) fusion(bf16[1536,2304]{0,1:T(8,128)(2,1)} %constant_dynamic-update-slice_fusion.13, bf16[768,768]{1,0:T(8,128)(2,1)S(1)} %bitcast.257, bf16[768,768]{1,0:T(8,128)(2,1)S(1)} %bitcast.259, bf16[768,768]{1,0:T(8,128)(2,1)S(1)} %bitcast.261), kind=kOutput, calls=%fused_computation.221 | convolution fusion | flops 5447613440 | bytes 15336960 | tf_op jit(solution)/shard_map/nc,dc->nd/dot_general | solution.py:466
  441.3 9.4 %convolution_convert_fusion.1 = bf16[768,2304]{1,0:T(8,128)(2,1)S(1)} fusion(bf16[1536,2304]{0,1:T(8,128)(2,1)} %constant_dynamic-update-slice_fusion.13, bf16[1536,768]{0,1:T(8,128)(2,1)S(1)} %copy-done.4, f32[768]{0:T(1024)S(1)} %copy-done.67, f32[768]{0:T(1024)S(1)} %copy-done.64, f32[1536]{0:T(1024)S(1)} %copy-done.58, f32[1536]{0:T(1024)S(1)} %copy-done.56), kind=kOutput, calls=%fused_computation.50 | convolution fusion | flops 5444665344 | bytes 12994560 | tf_op jit(solution)/shard_map/nd,nc->dc/dot_general | solution.py:462
  450.7 1.7 fusion.99
  453.0 6.2 %copy.111 = f32[1536,768]{0,1:T(8,128)} copy(f32[1536,768]{1,0:T(8,128)} %get-tuple-element.138) | data formatting | bytes 9437184 | tf_op jit(solution)/shard_map/nc,dc->nd/dot_general | solution.py:466
  459.3 3.3 fusion.25
  463.0 3.0 fusion.23
  469.6 7.0 %add_add_fusion.2 = f32[1536,768]{0,1:T(8,128)} fusion(f32[1536,768]{0,1:T(8,128)} %get-tuple-element.58, bf16[1536,768]{0,1:T(8,128)(2,1)} %copy.88, f32[1536]{0:T(1024)S(1)} %negate_multiply_fusion, f32[1536]{0:T(1024)} %copy-done.60, f32[1536]{0:T(1024)S(1)} %multiply_multiply_fusion.2, f32[1536]{0:T(1024)S(1)} %copy-done.56, ...), kind=kLoop, calls=%fused_computation.62 | loop fusion | flops 14155776 | bytes 18908160 | tf_op jit(solution)/shard_map/add | solution.py:469
  476.6 6.2 %copy.116 = f32[1536,768]{1,0:T(8,128)} copy(f32[1536,768]{0,1:T(8,128)} %add_add_fusion.2) | data formatting | bytes 9437184
  487.8 5.6 pad.20
  493.4 88.6 %shard_map.272 = f32[320,768]{1,0:T(8,128)S(1)} custom-call(bf16[2,2,2,2,2,320,768]{6,5,4,3,2,1,0:T(8,128)(2,1)} %bitcast.222), custom_call_target="tpu_custom_call" | custom-call | tf_op jit(solution)/shard_map/pallas_call | solution.py:220
  (280 shorter events, 64.1 us)
Async XLA Ops:
  21.5 201.3 %copy-start.3 = (bf16[1536,768]{0,1:T(8,128)(2,1)}, bf16[1536,768]{0,1:T(8,128)(2,1)S(1)}, u32[]{:S(2)}) copy-start(bf16[1536,768]{0,1:T(8,128)(2,1)S(1)} %copy.67) | copy-start | bytes 7077892
  21.9 118.0 %copy-start.55 = (f32[1536]{0:T(1024)}, f32[1536]{0:T(1024)S(1)}, u32[]{:S(2)}) copy-start(f32[1536]{0:T(1024)S(1)} %broadcast_multiply_fusion.1) | copy-start | bytes 18436
  22.5 102.3 %copy-start.61 = (f32[1536]{0:T(1024)}, f32[1536]{0:T(1024)S(1)}, u32[]{:S(2)}) copy-start(f32[1536]{0:T(1024)S(1)} %fusion.24) | copy-start | bytes 18436
  22.6 117.3 %copy-start.57 = (f32[1536]{0:T(1024)}, f32[1536]{0:T(1024)S(1)}, u32[]{:S(2)}) copy-start(f32[1536]{0:T(1024)S(1)} %fusion.82) | copy-start | bytes 18436
  126.9 12.9 %copy-start.63 = (f32[768]{0:T(1024)}, f32[768]{0:T(1024)S(1)}, u32[]{:S(2)}) copy-start(f32[768]{0:T(1024)S(1)} %reshape.394) | copy-start | bytes 9220
  127.8 12.1 %copy-start.66 = (f32[768]{0:T(1024)}, f32[768]{0:T(1024)S(1)}, u32[]{:S(2)}) copy-start(f32[768]{0:T(1024)S(1)} %reshape.395) | copy-start | bytes 9220
  139.8 7.8 %copy-start.39 = (bf16[32,24,768]{2,1,0:T(8,128)(2,1)}, bf16[32,24,768]{2,1,0:T(8,128)(2,1)S(1)}, u32[]{:S(2)}) copy-start(bf16[32,24,768]{2,1,0:T(8,128)(2,1)S(1)} %get-tuple-element.64) | copy-start | bytes 3538948
  139.8 7.8 %copy-start.41 = (bf16[32,24,768]{2,1,0:T(8,128)(2,1)}, bf16[32,24,768]{2,1,0:T(8,128)(2,1)S(1)}, u32[]{:S(2)}) copy-start(bf16[32,24,768]{2,1,0:T(8,128)(2,1)S(1)} %get-tuple-element.65) | copy-start | bytes 3538948
  139.8 7.8 %copy-start.43 = (bf16[32,24,768]{2,1,0:T(8,128)(2,1)}, bf16[32,24,768]{2,1,0:T(8,128)(2,1)S(1)}, u32[]{:S(2)}) copy-start(bf16[32,24,768]{2,1,0:T(8,128)(2,1)S(1)} %get-tuple-element.66) | copy-start | bytes 3538948
  165.3 51.3 %copy-start.16 = (bf16[2,256,1,12,64]{1,0,4,3,2:T(2,128)(2,1)}, bf16[2,256,1,12,64]{1,0,4,3,2:T(2,128)(2,1)S(1)}, u32[]{:S(2)}) copy-start(bf16[2,256,1,12,64]{1,0,4,3,2:T(2,128)(2,1)S(1)} %get-tuple-element.82) | copy-start | bytes 2359300
  203.7 2.2 copy-start.30
  203.7 4.5 copy-start.31
  205.9 3.5 copy-start.1
  212.1 3.4 copy-start.2
  212.1 2.2 copy-start.26
  217.9 3.8 copy-start
  217.9 2.2 copy-start.20
  223.0 2.5 copy-start.53
  225.5 2.7 copy-start.68
  228.2 22.5 %copy-start.9 = (bf16[1536,768]{1,0:T(8,128)(2,1)S(1)}, bf16[1536,768]{1,0:T(8,128)(2,1)}, u32[]{:S(2)}) copy-start(bf16[1536,768]{1,0:T(8,128)(2,1)} %param.18) | copy-start | bytes 7077892
  228.2 48.3 %slice-start.6 = ((s8[4718592]{0:T(1024)(128)(4,1)}), s8[524288]{0:T(1024)(128)(4,1)S(1)}, s32[]{:S(2)}) async-start(s8[4718592]{0:T(1024)(128)(4,1)} %bitcast.226), calls=%async_computation.6 | async-start | bytes 1048576
  250.8 25.8 %slice-start.7 = ((s8[4718592]{0:T(1024)(128)(4,1)}), s8[4194304]{0:T(1024)(128)(4,1)S(1)}, s32[]{:S(2)}) async-start(s8[4718592]{0:T(1024)(128)(4,1)} %bitcast.226), calls=%async_computation.7 | async-start | bytes 8388608
  250.8 25.8 %copy-start.69 = (f32[768]{0:T(1024)S(1)}, f32[768]{0:T(1024)}, u32[]{:S(2)}) copy-start(f32[768]{0:T(1024)} %reshape.402) | copy-start | bytes 9220
  302.7 5.1 copy-start.47
  302.8 5.1 copy-start.48
  302.8 18.5 %slice-start.8 = ((s8[4718592]{0:T(1024)(128)(4,1)}), s8[524288]{0:T(1024)(128)(4,1)S(1)}, s32[]{:S(2)}) async-start(s8[4718592]{0:T(1024)(128)(4,1)} %bitcast.228), calls=%async_computation.8 | async-start | bytes 1048576
  307.9 13.4 %slice-start.9 = ((s8[4718592]{0:T(1024)(128)(4,1)}), s8[4194304]{0:T(1024)(128)(4,1)S(1)}, s32[]{:S(2)}) async-start(s8[4718592]{0:T(1024)(128)(4,1)} %bitcast.228), calls=%async_computation.9 | async-start | bytes 8388608
  334.4 11.7 %slice-start.10 = ((s8[4718592]{0:T(1024)(128)(4,1)}), s8[524288]{0:T(1024)(128)(4,1)S(1)}, s32[]{:S(2)}) async-start(s8[4718592]{0:T(1024)(128)(4,1)} %bitcast.230), calls=%async_computation.10 | async-start | bytes 1048576
  340.9 5.2 slice-start.11
  340.9 6.4 %copy-start.7 = (f32[1536,768]{0,1:T(8,128)S(1)}, f32[1536,768]{0,1:T(8,128)}, u32[]{:S(2)}) copy-start(f32[1536,768]{0,1:T(8,128)} %copy.89) | copy-start | bytes 14155780
  347.3 4.1 copy-start.8
  350.7 4.0 copy-start.60
  351.3 3.3 copy-start.54
  354.6 3.1 copy-start.38
  354.6 3.8 copy-start.46
  362.1 3.6 copy-start.50
  365.7 8.1 %copy-start.52 = (f32[2,12,256]{2,1,0:T(8,128)S(1)}, f32[2,12,256]{2,1,0:T(8,128)}, u32[]{:S(2)}) copy-start(f32[2,12,256]{2,1,0:T(8,128)} %log_add_fusion.1) | copy-start | bytes 73732
  373.9 8.3 %copy-start.51 = (f32[2,12,256]{2,1,0:T(8,128)S(1)}, f32[2,12,256]{2,1,0:T(8,128)}, u32[]{:S(2)}) copy-start(f32[2,12,256]{2,1,0:T(8,128)} %log_add_fusion.2) | copy-start | bytes 73732
  382.1 4.9 copy-start.32
  382.1 12.0 %slice-start.2 = ((s8[6291456]{0:T(1024)(128)(4,1)}), s8[4194304]{0:T(1024)(128)(4,1)S(1)}, s32[]{:S(2)}) async-start(s8[6291456]{0:T(1024)(128)(4,1)} %bitcast.218), calls=%async_computation.2 | async-start | bytes 8388608
  387.0 7.1 %slice-start.3 = ((s8[6291456]{0:T(1024)(128)(4,1)}), s8[2097152]{0:T(1024)(128)(4,1)S(1)}, s32[]{:S(2)}) async-start(s8[6291456]{0:T(1024)(128)(4,1)} %bitcast.218), calls=%async_computation.3 | async-start | bytes 4194304
  387.0 16.5 %slice-start.4 = ((s8[6291456]{0:T(1024)(128)(4,1)}), s8[4194304]{0:T(1024)(128)(4,1)S(1)}, s32[]{:S(2)}) async-start(s8[6291456]{0:T(1024)(128)(4,1)} %bitcast.220), calls=%async_computation.4 | async-start | bytes 8388608
  394.1 9.4 %slice-start.5 = ((s8[6291456]{0:T(1024)(128)(4,1)}), s8[2097152]{0:T(1024)(128)(4,1)S(1)}, s32[]{:S(2)}) async-start(s8[6291456]{0:T(1024)(128)(4,1)} %bitcast.220), calls=%async_computation.5 | async-start | bytes 4194304
  398.7 3.3 copy-start.29
  398.7 4.8 copy-start.27
  412.8 6.3 %slice-start = ((s8[6291456]{0:T(1024)(128)(4,1)}), s8[4194304]{0:T(1024)(128)(4,1)S(1)}, s32[]{:S(2)}) async-start(s8[6291456]{0:T(1024)(128)(4,1)} %bitcast.216), calls=%async_computation | async-start | bytes 8388608
  415.7 3.3 slice-start.1
  415.7 3.3 copy-start.21
  428.9 2.8 copy-start.44
  431.7 9.5 %copy-start.4 = (bf16[1536,768]{0,1:T(8,128)(2,1)S(1)}, bf16[1536,768]{0,1:T(8,128)(2,1)}, u32[]{:S(2)}) copy-start(bf16[1536,768]{0,1:T(8,128)(2,1)} %copy-done.3) | copy-start | bytes 7077892
  431.7 9.5 %copy-start.56 = (f32[1536]{0:T(1024)S(1)}, f32[1536]{0:T(1024)}, u32[]{:S(2)}) copy-start(f32[1536]{0:T(1024)} %copy-done.55) | copy-start | bytes 18436
  431.7 9.5 %copy-start.58 = (f32[1536]{0:T(1024)S(1)}, f32[1536]{0:T(1024)}, u32[]{:S(2)}) copy-start(f32[1536]{0:T(1024)} %copy-done.57) | copy-start | bytes 18436
  431.7 9.5 %copy-start.64 = (f32[768]{0:T(1024)S(1)}, f32[768]{0:T(1024)}, u32[]{:S(2)}) copy-start(f32[768]{0:T(1024)} %copy-done.63) | copy-start | bytes 9220
  431.7 9.5 %copy-start.67 = (f32[768]{0:T(1024)S(1)}, f32[768]{0:T(1024)}, u32[]{:S(2)}) copy-start(f32[768]{0:T(1024)} %copy-done.66) | copy-start | bytes 9220
  459.2 3.3 copy-start.62
  459.3 3.8 copy-start.5
  459.3 3.8 copy-start.59
  459.3 3.8 copy-start.65
  476.6 7.0 %copy-start.15 = (bf16[768,768]{1,0:T(8,128)(2,1)S(1)}, bf16[768,768]{1,0:T(8,128)(2,1)}, u32[]{:S(2)}) copy-start(bf16[768,768]{1,0:T(8,128)(2,1)} %get-tuple-element.76) | copy-start | bytes 3538948
  476.6 7.1 %copy-start.14 = (bf16[768,768]{1,0:T(8,128)(2,1)S(1)}, bf16[768,768]{1,0:T(8,128)(2,1)}, u32[]{:S(2)}) copy-start(bf16[768,768]{1,0:T(8,128)(2,1)} %get-tuple-element.75) | copy-start | bytes 3538948
  483.7 2.3 copy-start.12
  483.7 3.6 slice-start.12
  483.8 2.3 copy-start.11
  485.0 2.4 slice-start.13
  (21 other events, 32.9 us)

commit v2 on v1

--- a/solution.py
+++ b/solution.py
@@ -5,6 +5,7 @@
 import jax.numpy as jnp
 from jax import lax
 from jax.experimental import pallas as pl
+from jax.experimental.layout import Layout, with_layout_constraint
 from jax.experimental.pallas import tpu as pltpu
 from jax.sharding import PartitionSpec as P
 
@@ -15,6 +16,96 @@
 
 EPSILON = 1e-05
 CHUNK = 32
+LANES = 128
+
+
+def dot32(left, right, left_dim, right_dim):
+    return lax.dot_general(
+        left, right, (((left_dim,), (right_dim,)), ((), ())), preferred_element_type=jnp.float32
+    )
+
+
+def mask_bias(seg_rows, seg_columns):
+    row = lax.broadcasted_iota(jnp.int32, (LEN, LEN), 0)
+    column = lax.broadcasted_iota(jnp.int32, (LEN, LEN), 1)
+    allowed = jnp.logical_and(seg_rows == seg_columns, column <= row)
+    return jnp.where(allowed, 0.0, -1e30).astype(jnp.float32)
+
+
+def one_head(values, first):
+    lane = lax.broadcasted_iota(jnp.int32, values.shape, 1)
+    return jnp.where((lane < LANES // 2) == first, values, jnp.zeros_like(values))
+
+
+def softmax_rows(queries, key_rows, bias):
+    scores = dot32(queries, key_rows, 1, 1) * (1.0 / math.sqrt(D // HEADS)) + bias
+    exponent = jnp.exp(scores - jnp.max(scores, axis=-1, keepdims=True))
+    return exponent * (1.0 / jnp.sum(exponent, axis=-1, keepdims=True))
+
+
+def attend_kernel(row_ref, column_ref, qkv_ref, out_ref, bias):
+    bias[...] = mask_bias(row_ref[0], column_ref[0])
+    for at in range(0, D, LANES):
+        queries = qkv_ref[:, at : at + LANES]
+        key_rows = qkv_ref[:, D + at : D + at + LANES]
+        value_rows = qkv_ref[:, 2 * D + at : 2 * D + at + LANES]
+        total = None
+        for first in (True, False):
+            probs = softmax_rows(one_head(queries, first), key_rows, bias[...])
+            mixed = dot32(probs.astype(jnp.bfloat16), one_head(value_rows, first), 1, 0)
+            total = mixed if total is None else total + mixed
+        out_ref[:, at : at + LANES] = total.astype(jnp.bfloat16)
+
+
+def attend_back_kernel(row_ref, column_ref, qkv_ref, grad_ref, out_ref, bias):
+    bias[...] = mask_bias(row_ref[0], column_ref[0])
+    low16 = jnp.bfloat16
+    scale = 1.0 / math.sqrt(D // HEADS)
+    for at in range(0, D, LANES):
+        queries = qkv_ref[:, at : at + LANES]
+        key_rows = qkv_ref[:, D + at : D + at + LANES]
+        value_rows = qkv_ref[:, 2 * D + at : 2 * D + at + LANES]
+        grad = grad_ref[:, at : at + LANES]
+        totals = None
+        for first in (True, False):
+            query_one = one_head(queries, first)
+            grad_one = one_head(grad, first)
+            probs = softmax_rows(query_one, key_rows, bias[...])
+            grad_probs = dot32(grad_one, value_rows, 1, 1)
+            inner = jnp.sum(probs * grad_probs, axis=-1, keepdims=True)
+            grad_scores = (probs * (grad_probs - inner)).astype(low16)
+            parts = (
+                dot32(grad_scores, one_head(key_rows, first), 1, 0),
+                dot32(grad_scores, query_one, 0, 0),
+                dot32(probs.astype(low16), grad_one, 0, 0),
+            )
+            totals = parts if totals is None else tuple(a + b for a, b in zip(totals, parts))
+        out_ref[:, at : at + LANES] = (totals[0] * scale).astype(low16)
+        out_ref[:, D + at : D + at + LANES] = (totals[1] * scale).astype(low16)
+        out_ref[:, 2 * D + at : 2 * D + at + LANES] = totals[2].astype(low16)
+
+
+def per_sequence(kernel, segments, arrays, width):
+    count = segments.shape[0]
+
+    def whole(columns):
+        return pl.BlockSpec((LEN, columns), lambda i: (i, 0))
+
+    return pl.pallas_call(
+        kernel,
+        grid=(count,),
+        out_shape=jax.ShapeDtypeStruct((count * LEN, width), jnp.bfloat16),
+        in_specs=[
+            pl.BlockSpec((1, LEN, 1), lambda i: (i, 0, 0)),
+            pl.BlockSpec((1, 1, LEN), lambda i: (i, 0, 0)),
+        ]
+        + [whole(array.shape[1]) for array in arrays],
+        out_specs=whole(width),
+        scratch_shapes=[pltpu.VMEM((LEN, LEN), jnp.float32)],
+        compiler_params=pltpu.CompilerParams(vmem_limit_bytes=32 * 1024 * 1024),
+    )(segments[:, :, None], segments[:, None, :], *arrays)
+
+
 AXES = ("fsdp", "rep")
 PLACES = ("zh", "zl", "x", "c", "y")
 MESH = pl.DeviceIdType.MESH
@@ -43,7 +134,8 @@
 
 def gather_kernel(chunk, block_ref, all_ref, send_sem, recv_sem, own_sem):
     where, partner = places_and_partners()
-    chunks = block_ref.shape[0] // chunk
+    total_rows = block_ref.shape[0]
+    chunks = -(-total_rows // chunk)
     own = pltpu.make_async_copy(
         block_ref, all_ref.at[tuple(where[name] for name in PLACES)], own_sem
     )
@@ -54,7 +146,7 @@
 
     def begin(number, step):
         order = orders[number % 2]
-        rows = pl.ds(number * chunk, chunk)
+        rows = pl.ds(number * chunk, min(chunk, total_rows - number * chunk))
         index = tuple(
             slice(None) if name in order[:step] else where[name] for name in PLACES
         ) + (rows,)
@@ -70,14 +162,14 @@
         copy.start()
         copies[number, step] = copy
 
-    pairs = chunks // 2
+    pairs = -(-chunks // 2)
     steps = len(PLACES)
     for wave in range(pairs + steps):
         for pair in range(pairs):
             step = wave - pair
             if not 0 <= step <= steps:
                 continue
-            for number in (2 * pair, 2 * pair + 1):
+            for number in range(2 * pair, min(2 * pair + 2, chunks)):
                 if step == 1 and number == 0:
                     own.wait()
                 if step > 0:
@@ -90,7 +182,7 @@
 
 def gather_all(block, chunk):
     rows, width = block.shape
-    chunks = rows // chunk
+    chunks = -(-rows // chunk)
     return pl.pallas_call(
         functools.partial(gather_kernel, chunk),
         out_shape=jax.ShapeDtypeStruct((2,) * 5 + (rows, width), block.dtype),
@@ -109,13 +201,14 @@
     chunk, parts_ref, sum_ref, held, got0, got1, got2, got3, got4, send_sem, recv_sem, own_sem
 ):
     where, partner = places_and_partners()
-    chunks = parts_ref.shape[5] // chunk
+    total_rows = parts_ref.shape[5]
+    chunks = -(-total_rows // chunk)
     zh, zl, x, c, y = (where[name] for name in PLACES)
     everything = slice(None)
     f32 = jnp.float32
 
     def rows_of(number):
-        return pl.ds(number * chunk, chunk)
+        return pl.ds(number * chunk, min(chunk, total_rows - number * chunk))
 
     own = []
     for number in range(chunks):
@@ -199,13 +292,13 @@
 
     for number in range(chunks):
         begin(number, 0)
-    pairs = chunks // 2
+    pairs = -(-chunks // 2)
     for wave in range(1, pairs + 5):
         for pair in range(pairs):
             step = wave - pair
             if not 1 <= step <= 5:
                 continue
-            for number in (2 * pair, 2 * pair + 1):
+            for number in range(2 * pair, min(2 * pair + 2, chunks)):
                 add(number, step - 1)
                 if step < 5:
                     begin(number, step)
@@ -215,7 +308,7 @@
 
 def scatter_sum(parts, chunk):
     rows, width = parts.shape[5:]
-    chunks = rows // chunk
+    chunks = -(-rows // chunk)
     low = parts.dtype
     return pl.pallas_call(
         functools.partial(scatter_kernel, chunk),
@@ -252,7 +345,7 @@
     small = jnp.pad(small, (0, D - small.shape[0]))[None]
     pieces = columns_to_rows(wq) + [wo] + columns_to_rows(wu) + [wd, small]
     used = sum(piece.shape[0] for piece in pieces)
-    rows = -(-used // (2 * CHUNK)) * 2 * CHUNK
+    rows = -(-used // 16) * 16
     block = jnp.pad(jnp.concatenate(pieces, axis=0), ((0, rows - used), (0, 0)))
     whole = gather_all(block, CHUNK).reshape(count, rows, D)
     n, m = wq.shape[0], wd.shape[0]
@@ -290,7 +383,7 @@
         for part in columns_to_rows(weight.astype(low16))
     ] + [wd.astype(low16).reshape(count, m, D), small]
     used = sum(piece.shape[1] for piece in pieces)
-    rows = -(-used // (2 * CHUNK)) * 2 * CHUNK
+    rows = -(-used // 16) * 16
     parts = jnp.pad(jnp.concatenate(pieces, axis=1), ((0, 0), (0, rows - used), (0, 0)))
     total = scatter_sum(parts.reshape((2,) * 5 + (rows, D)), CHUNK)
     at = 0
@@ -323,16 +416,8 @@
     )
 
 
-def block_mask(seg_block):
-    places = jnp.arange(seg_block.shape[1])
-    causal = places[None, :] <= places[:, None]
-    same_doc = seg_block[:, :, None] == seg_block[:, None, :]
-    return jnp.logical_and(same_doc, causal[None])
-
-
-def masked_scores(queries, key_rows, allowed, score_scale):
-    raw = jnp.einsum("sqhd,skhd->shqk", queries, key_rows, preferred_element_type=jnp.float32)
-    return jnp.where(allowed[:, None], raw * score_scale, -1e30)
+def by_rows(values):
+    return with_layout_constraint(values, Layout(major_to_minor=(0, 1)))
 
 
 def local(
@@ -374,37 +459,15 @@
     ) = gathered
     f32 = jnp.float32
     low16 = jnp.bfloat16
-    seq_count = segments.shape[0]
-    seq_span = min(seq_count, max(1, 512 // LEN))
-    block_count = seq_count // seq_span
-    head_dim = D // HEADS
-    score_scale = 1.0 / math.sqrt(head_dim)
     rows_in = tokens.astype(f32)
     normed16 = norm_rows(rows_in, gain_attn.astype(f32), shift_attn.astype(f32)).astype(low16)
     qkv_bias = jnp.concatenate(
         [bias_query.astype(f32), jnp.zeros((D,), f32), bias_value.astype(f32)]
     )
     qkv16 = (jnp.dot(normed16, mat_qkv, preferred_element_type=f32) + qkv_bias).astype(low16)
-    heads_view = qkv16.reshape(seq_count, LEN, 3, HEADS, head_dim)
-    attn_parts = []
-    lse_parts = []
-    for number in range(block_count):
-        first_seq = number * seq_span
-        current = heads_view[first_seq : first_seq + seq_span]
-        allowed = block_mask(segments[first_seq : first_seq + seq_span])
-        scores = masked_scores(current[:, :, 0], current[:, :, 1], allowed, score_scale)
-        row_max = jnp.max(scores, axis=-1, keepdims=True)
-        exponent = jnp.exp(scores - row_max)
-        totals = jnp.sum(exponent, axis=-1, keepdims=True)
-        probs_low = (exponent / totals).astype(low16)
-        lse_parts.append(row_max + jnp.log(totals))
-        mixed = jnp.einsum(
-            "shqk,skhd->sqhd", probs_low, current[:, :, 2], preferred_element_type=f32
-        )
-        attn_parts.append(mixed.reshape(seq_span * LEN, D))
-    attended16 = jnp.concatenate(attn_parts, axis=0).astype(low16)
+    attended16 = per_sequence(attend_kernel, segments, (qkv16,), D)
     branch = jnp.dot(attended16, mat_out, preferred_element_type=f32) + bias_out.astype(f32)
-    resid = rows_in + branch
+    resid = by_rows(rows_in + branch)
     normed_mlp16 = norm_rows(resid, gain_mlp.astype(f32), shift_mlp.astype(f32)).astype(low16)
     hidden_pre = jnp.dot(normed_mlp16, mat_up, preferred_element_type=f32) + bias_up.astype(f32)
     hidden16 = gelu_tanh(hidden_pre).astype(low16)
@@ -418,52 +481,22 @@
     grad_pre16 = gelu_pull(grad_hidden)[0].astype(low16)
     grad_up_weight = jnp.einsum("nd,nf->df", normed_mlp16, grad_pre16, preferred_element_type=f32)
     grad_up_bias = jnp.sum(grad_pre16.astype(f32), axis=0)
-    grad_normed_mlp = jnp.einsum("nf,df->nd", grad_pre16, mat_up, preferred_element_type=f32)
+    grad_normed_mlp = by_rows(jnp.einsum("nf,df->nd", grad_pre16, mat_up, preferred_element_type=f32))
     unused, second_pull = jax.vjp(norm_rows, resid, gain_mlp.astype(f32), shift_mlp.astype(f32))
     grad_resid_part, grad_mlp_gain, grad_mlp_shift = second_pull(grad_normed_mlp)
-    grad_resid = grad_out + grad_resid_part
+    grad_resid = by_rows(grad_out + grad_resid_part)
     grad_branch16 = grad_resid.astype(low16)
     grad_out_weight = jnp.einsum("ne,nd->ed", attended16, grad_branch16, preferred_element_type=f32)
     grad_out_bias = jnp.sum(grad_branch16.astype(f32), axis=0)
     grad_attended16 = jnp.einsum(
         "nd,ed->ne", grad_branch16, mat_out, preferred_element_type=f32
     ).astype(low16)
-    grad_heads = grad_attended16.reshape(seq_count, LEN, HEADS, head_dim)
-    grad_parts = []
-    for number in range(block_count):
-        first_seq = number * seq_span
-        current = heads_view[first_seq : first_seq + seq_span]
-        allowed = block_mask(segments[first_seq : first_seq + seq_span])
-        scores = masked_scores(current[:, :, 0], current[:, :, 1], allowed, score_scale)
-        probs = jnp.exp(scores - lse_parts[number])
-        probs_low = probs.astype(low16)
-        grad_block = grad_heads[first_seq : first_seq + seq_span]
-        grad_probs = jnp.einsum(
-            "sqhd,skhd->shqk", grad_block, current[:, :, 2], preferred_element_type=f32
-        )
-        grad_value = jnp.einsum(
-            "shqk,sqhd->skhd", probs_low, grad_block, preferred_element_type=f32
-        )
-        inner = jnp.sum(probs * grad_probs, axis=-1, keepdims=True)
-        grad_scores = (probs * (grad_probs - inner)).astype(low16)
-        grad_query = (
-            jnp.einsum("shqk,skhd->sqhd", grad_scores, current[:, :, 1], preferred_element_type=f32)
-            * score_scale
-        )
-        grad_key = (
-            jnp.einsum("shqk,sqhd->skhd", grad_scores, current[:, :, 0], preferred_element_type=f32)
-            * score_scale
-        )
-        stacked = jnp.stack([grad_query, grad_key, grad_value], axis=2).reshape(
-            seq_span * LEN, 3 * D
-        )
-        grad_parts.append(stacked.astype(low16))
-    grad_qkv16 = jnp.concatenate(grad_parts, axis=0)
+    grad_qkv16 = per_sequence(attend_back_kernel, segments, (qkv16, grad_attended16), 3 * D)
     grad_qkv_weight = jnp.einsum("nd,nc->dc", normed16, grad_qkv16, preferred_element_type=f32)
     bias_sums = jnp.sum(grad_qkv16.astype(f32), axis=0)
     grad_query_bias = bias_sums[:D]
     grad_value_bias = bias_sums[2 * D :]
-    grad_normed = jnp.einsum("nc,dc->nd", grad_qkv16, mat_qkv, preferred_element_type=f32)
+    grad_normed = by_rows(jnp.einsum("nc,dc->nd", grad_qkv16, mat_qkv, preferred_element_type=f32))
     unused, first_pull = jax.vjp(norm_rows, rows_in, gain_attn.astype(f32), shift_attn.astype(f32))
     grad_rows_part, grad_attn_gain, grad_attn_shift = first_pull(grad_normed)
     grad_tokens = grad_resid + grad_rows_part

time: 592 us -> 455 us (0.77)
  local copies, waits for them, and re-layouts: 175 us -> 56.9 us
  matrix products: 175 us -> 133 us
  Pallas kernels: 187 us -> 227 us
  other arithmetic: 47.3 us -> 32.4 us
    slice x18 -> x0, local copies, waits for them, and re-layouts: 67.3 us -> none  [the longest x7 34.4 us: local(): current = heads_view[first_seq:first_seq + seq_span]]
    pallas_call x0 -> x2, Pallas kernels: none -> 42.5 us  [per_sequence(): pl.pallas_call(kernel, grid=(count,), out_shape=jax.ShapeDtypeStruct((cou...]
    dot_general x18 -> x0, matrix products: 41 us -> none  [the longest x3 14.3 us: local(): jnp.einsum('shqk,sqhd->skhd', probs_low, grad_block, preferred_element_ty...]
    unnamed x203 -> x115, local copies, waits for them, and re-layouts: 40.7 us -> 11.3 us
    dot_general x2 -> x0, local copies, waits for them, and re-layouts: 12.7 us -> none  [the longest x1 6.48 us: local(): jnp.einsum('nf,df->nd', grad_pre16, mat_up, preferred_element_type=f32)]
    convert_element_type x3 -> x0, other arithmetic: 7.98 us -> none  [local(): grad_scores = (probs * (grad_probs - inner)).astype(low16)]
    another operation x3 -> x0, local copies, waits for them, and re-layouts: 7.41 us -> none  [local(): jnp.stack([grad_query, grad_key, grad_value], axis=2)]
    reduce_sum x3 -> x1, other arithmetic: 11.4 us -> 4.71 us  [norm_rows(): return center * lax.rsqrt(spread + EPSILON) * gain + shift]
where the time goes in v2:
time: 455 us; the launch traced here: 451 us
  Pallas kernels  227 us (50%)
  matrix products  133 us (29%)
  local copies, waits for them, and re-layouts  56.9 us (13%)
  other arithmetic  32.4 us (7%)
    pallas_call x1, Pallas kernels, gather_all(): pl.pallas_call(functools.partial(gather_kernel, chunk), out_shape=jax.Sha...  96.1 us
    pallas_call x1, Pallas kernels, scatter_sum(): pl.pallas_call(functools.partial(scatter_kernel, chunk), out_shape=jax.Sh...  88.1 us
    pallas_call x2, Pallas kernels, per_sequence(): pl.pallas_call(kernel, grid=(count,), out_shape=jax.ShapeDtypeStruct((cou...  42.5 us
    dot_general x1, matrix products, local(): jnp.einsum('nd,fd->nf', cotangent, mat_down, preferred_element_type=f32)  28.4 us
    dot_general x1, matrix products, local(): jnp.dot(normed_mlp16, mat_up, preferred_element_type=f32)  21.9 us
    dot_general x1, matrix products, local(): jnp.einsum('nf,df->nd', grad_pre16, mat_up, preferred_element_type=f32)  15.3 us
    dot_general x1, matrix products, local(): jnp.einsum('nc,dc->nd', grad_qkv16, mat_qkv, preferred_element_type=f32)  12.6 us
    dot_general x1, matrix products, local(): jnp.einsum('nd,nf->df', normed_mlp16, grad_pre16, preferred_element_type=...  11.5 us

profile of v2, /device:TPU:0, one launch (start us, length us, event | category | flops | bytes accessed | tf_op | source)
XLA Modules:
  0.0 451.0 jit_solution(6700208078405601626)
XLA Ops:
  0.7 6.2 %concatenate.28 = bf16[288]{0:T(512)(128)(2,1)S(1)} concatenate(bf16[24]{0:T(256)(128)(2,1)} %param.19, bf16[24]{0:T(256)(128)(2,1)} %param.20, bf16[24]{0:T(256)(128)(2,1)} %param.22, bf16[24]{0:T(256)(128)(2,1)} %param.23, bf16[24]{0:T(256)(128)(2,1)} %param.25, bf16[24]{0:T(256)(128)(2,1)} %param.26, bf16[24]{0:T(256)(128)(2,1)} %param.27, bf16[24]{0:T(256)(128)(2,1)} %param.31, ...), dimensions={0} | concatenate | bytes 1152 | tf_op jit(solution)/shard_map/concatenate | solution.py:344
  6.9 0.7 broadcast_in_dim.17.column_ref
  7.6 2.0 convert_reduce_fusion
  9.6 2.5 fusion.18
  12.4 0.4 copy-done.31
  12.7 0.8 pad.18.block_ref
  13.5 0.3 copy.32.row_ref
  13.9 96.1 %shard_map.271 = bf16[2,2,2,2,2,304,768]{6,5,4,3,2,1,0:T(8,128)(2,1)} custom-call(bf16[304,768]{1,0:T(8,128)(2,1)} %pad.18.block_ref), custom_call_target="tpu_custom_call" | custom-call | tf_op jit(solution)/shard_map/pallas_call | solution.py:186
  109.9 1.1 slice.276
  112.0 4.8 %slice.293 = bf16[32,96,768]{2,1,0:T(8,128)(2,1)} slice(bf16[32,304,768]{2,1,0:T(8,128)(2,1)} %bitcast.77), slice={[0:32], [192:288], [0:768]} | slice | bytes 9437184 | tf_op jit(solution)/shard_map/slice | solution.py:361
  116.8 7.1 %fusion.37 = (bf16[32,24,768]{2,1,0:T(8,128)(2,1)}, bf16[32,24,768]{2,1,0:T(8,128)(2,1)}, bf16[32,24,768]{2,1,0:T(8,128)(2,1)}, bf16[32,24,768]{2,1,0:T(8,128)(2...) fusion(bf16[32,304,768]{2,1,0:T(8,128)(2,1)} %bitcast.78), kind=kLoop, calls=%fused_computation.112 | loop fusion | bytes 18874368 | tf_op jit(solution)/shard_map/slice | solution.py:356
  123.9 1.0 copy-done.16
  124.9 0.4 copy-done.18
  125.3 6.2 %add_convert_fusion.qkv_ref = bf16[1536,2304]{1,0:T(8,128)(2,1)S(1)} fusion(f32[2304]{0:T(1024)S(1)} %pad_maximum_fusion.8, bf16[768,768]{1,0:T(8,128)(2,1)S(1)} %bitcast.95, bf16[768,768]{1,0:T(8,128)(2,1)S(1)} %bitcast.97, bf16[768,768]{1,0:T(8,128)(2,1)S(1)} %bitcast.99, bf16[1536,768]{1,0:T(8,128)(2,1)S(1)} %copy-done.5, f32[768]{0:T(1024)S(1)} %reshape.309, ...), kind=kOutput, calls=%fused_computation.16 | convolution fusion | flops 5460590592 | bytes 13003776 | tf_op jit(solution)/shard_map/dot_general | solution.py:467
  131.5 15.3 %shard_map.272 = bf16[1536,768]{1,0:T(8,128)(2,1)S(1)} custom-call(s32[6,256,1]{2,1,0:T(8,128)S(1)} %copy.32.row_ref, s32[6,1,256]{2,1,0:T(1,128)S(1)} %broadcast_in_dim.17.column_ref, bf16[1536,2304]{1,0:T(8,128)(2,1)S(1)} %add_convert_fusion.qkv_ref), custom_call_target="tpu_custom_call" | custom-call | tf_op jit(solution)/shard_map/pallas_call | solution.py:94
  146.8 2.3 fusion.42
  149.2 2.2 copy-done.7
  151.4 0.7 multiply_reduce_fusion.2
  152.1 21.9 %multiply_convert_fusion = (bf16[1536,3072]{1,0:T(8,128)(2,1)}, f32[1536,3072]{1,0:T(8,128)}) fusion(f32[3072]{0:T(1024)S(1)} %reshape.315, bf16[768,768]{1,0:T(8,128)(2,1)} %bitcast.105, bf16[768,768]{1,0:T(8,128)(2,1)} %bitcast.107, bf16[768,768]{1,0:T(8,128)(2,1)} %bitcast.109, bf16[768,768]{1,0:T(8,128)(2,1)} %bitcast.103, f32[1536,768]{1,0:T(8,128)} %copy-done.7, ...), kind=kOutput, calls=%fused_computation.15 | convolution fusion | flops 7319715840 | bytes 37779456 | tf_op jit(solution)/shard_map/dot_general | solution.py:472
  174.0 28.4 %fusion.43 = (bf16[3072]{0:T(1024)(128)(2,1)S(1)}, bf16[1536,3072]{1,0:T(8,128)(2,1)}) fusion(bf16[3072,768]{1,0:T(8,128)(2,1)} %bitcast.93, bf16[1536,768]{1,0:T(8,128)(2,1)} %param.18, f32[1536,3072]{1,0:T(8,128)} %get-tuple-element.71, f32[3072]{0:T(1024)S(1)} %reshape.315), kind=kOutput, calls=%fused_computation.118 | convolution fusion | flops 7370437632 | bytes 35407872 | tf_op jit(solution)/shard_map/nd,fd->nf/dot_general | solution.py:479
  202.5 11.2 %add_convert_fusion.1 = bf16[1536,768]{1,0:T(8,128)(2,1)} fusion(f32[1536,768]{1,0:T(8,128)S(1)} %bitcast.80, bf16[1536,3072]{1,0:T(8,128)(2,1)S(1)} %copy-done.39, bf16[3072,768]{1,0:T(8,128)(2,1)} %bitcast.94, f32[768]{0:T(1024)S(1)} %reshape.316), kind=kOutput, calls=%fused_computation.41 | convolution fusion | flops 7251296256 | bytes 21236736 | tf_op jit(solution)/shard_map/dot_general | solution.py:474
  213.7 9.9 %convolution_convert_fusion = bf16[3072,768]{1,0:T(8,128)(2,1)} fusion(bf16[1536,3072]{1,0:T(8,128)(2,1)S(1)} %copy-done.39, bf16[1536,768]{1,0:T(8,128)(2,1)S(1)} %copy-done.8), kind=kOutput, calls=%fused_computation.28 | convolution fusion | flops 7250116608 | bytes 16515072 | tf_op jit(solution)/shard_map/nf,nd->fd/dot_general | solution.py:477
  223.6 0.7 reshape.306
  224.3 15.3 %multiply_reduce_fusion = (bf16[768]{0:T(1024)(128)(2,1)S(1)}, f32[1536]{0:T(1024)S(1)}, bf16[768]{0:T(1024)(128)(2,1)S(1)}, f32[1536,768]{1,0:T(8,128)S(1)}) fusion(f32[1536,768]{1,0:T(8,128)} %copy-done.7, f32[1536]{0:T(1024)S(1)} %fusion.25, f32[1536]{0:T(1024)S(1)} %broadcast_multiply_fusion, f32[768]{0:T(1024)S(1)} %reshape.313, ...), kind=kOutput, calls=%fused_computation.37 | convolution fusion | flops 7276065792 | bytes 23617536 | tf_op jit(solution)/shard_map/nf,df->nd/dot_general | solution.py:484
  239.6 11.5 %convolution_convert_fusion.2 = bf16[768,3072]{1,0:T(8,128)(2,1)S(1)} fusion(bf16[1536,3072]{1,0:T(8,128)(2,1)} %get-tuple-element.75, f32[1536,768]{1,0:T(8,128)S(1)} %bitcast.82, f32[768]{0:T(1024)S(1)} %reshape.314, f32[768]{0:T(1024)S(1)} %reshape.313, f32[1536]{0:T(1024)S(1)} %fusion.25, f32[1536]{0:T(1024)S(1)} %broadcast_multiply_fusion), kind=kOutput, calls=%fused_computation.30 | convolution fusion | flops 7256014848 | bytes 18892800 | tf_op jit(solution)/shard_map/nd,nf->df/dot_general | solution.py:482
  251.2 3.4 fusion.36
  254.6 2.3 fusion.38
  256.9 0.7 reshape.303
  257.6 0.7 reshape.304
  258.3 4.8 %fusion.34 = (bf16[768]{0:T(1024)(128)(2,1)S(1)}, bf16[1536,768]{1,0:T(8,128)(2,1)S(1)}, bf16[768]{0:T(1024)(128)(2,1)S(1)}) fusion(f32[1536,768]{1,0:T(8,128)} %get-tuple-element.25, f32[1536]{0:T(1024)S(1)} %negate_multiply_fusion.1, bf16[1536,768]{1,0:T(8,128)(2,1)} %param.18), kind=kLoop, calls=%fused_computation.110 | loop fusion | flops 7076352 | bytes 9446400 | tf_op jit(solution)/shard_map/reduce_sum | solution.py:490
  263.1 3.1 convolution_convert_fusion.4
  266.2 0.7 reshape.302
  266.9 0.7 reshape.305
  267.6 4.2 convolution_convert_fusion.3.grad_ref
  271.8 27.2 %shard_map.273 = bf16[1536,2304]{1,0:T(8,128)(2,1)S(1)} custom-call(s32[6,256,1]{2,1,0:T(8,128)S(1)} %copy-done.4, s32[6,1,256]{2,1,0:T(1,128)S(1)} %broadcast_in_dim.17.column_ref, bf16[1536,2304]{1,0:T(8,128)(2,1)S(1)} %bitcast.74, bf16[1536,768]{1,0:T(8,128)(2,1)S(1)} %convolution_convert_fusion.3.grad_ref), custom_call_target="tpu_custom_call" | custom-call | tf_op jit(solution)/shard_map/pallas_call | solution.py:94
  299.0 2.9 copy-done.1
  301.9 4.8 %reduce = bf16[2304]{0:T(1024)(128)(2,1)} reduce(bf16[1536,2304]{1,0:T(8,128)(2,1)} %copy-done.1, bf16[]{:T(256)} %constant.24.clone.1), dimensions={0}, to_apply=%region_10.11.clone | reduce | flops 3536640 | bytes 7082498 | tf_op jit(solution)/shard_map/reduce_sum | solution.py:496
  306.7 1.3 fusion.41
  308.0 1.4 reshape.301
  309.3 0.7 reshape.300
  310.1 12.6 %fusion.33 = (bf16[768]{0:T(1024)(128)(2,1)}, f32[1536]{0:T(1024)S(1)}, f32[1536,768]{1,0:T(8,128)}) fusion(f32[768]{0:T(1024)S(1)} %copy-done.34, f32[1536]{0:T(1024)S(1)} %copy-done.25, bf16[1536,768]{1,0:T(8,128)(2,1)S(1)} %copy-done.6, bf16[1536,2304]{1,0:T(8,128)(2,1)} %copy-done.1, bf16[768,768]{1,0:T(8,128)(2,1)S(1)} %bitcast.96, ...), kind=kOutput, calls=%fused_computation.109 | convolution fusion | flops 5453510144 | bytes 17711616 | tf_op jit(solution)/shard_map/nc,dc->nd/dot_general | solution.py:499
  322.7 6.6 %convolution_convert_fusion.1 = bf16[768,2304]{1,0:T(8,128)(2,1)S(1)} fusion(bf16[1536,2304]{1,0:T(8,128)(2,1)S(1)} %copy-done.2, bf16[1536,768]{1,0:T(8,128)(2,1)S(1)} %copy-done.6, f32[768]{0:T(1024)S(1)} %copy-done.38, f32[768]{0:T(1024)S(1)} %copy-done.34, f32[1536]{0:T(1024)S(1)} %copy-done.29, f32[1536]{0:T(1024)S(1)} %copy-done.25), kind=kOutput, calls=%fused_computation.29 | convolution fusion | flops 5444665344 | bytes 12994560 | tf_op jit(solution)/shard_map/nd,nc->dc/dot_general | solution.py:495
  329.4 1.6 fusion.39
  331.0 1.4 reshape.299
  332.4 4.7 %fusion.17 = (bf16[768]{0:T(1024)(128)(2,1)}, f32[1536]{0:T(1024)}) fusion(f32[1536,768]{1,0:T(8,128)} %get-tuple-element.73, bf16[1536,768]{1,0:T(8,128)(2,1)S(1)} %copy-done.6, f32[1536]{0:T(1024)} %copy-done.28, f32[1536]{0:T(1024)S(1)} %copy-done.25, f32[1536]{0:T(1024)S(1)} %multiply_multiply_fusion.2, f32[768]{0:T(1024)} %copy-done.33), kind=kLoop, calls=%fused_computation.33 | loop fusion | flops 12973824 | bytes 7107072 | tf_op jit(solution)/shard_map/transpose(jvp())/reduce_sum | solution.py:408
  337.1 1.4 reshape.298
  338.5 1.5 concatenate.33
  340.0 0.7 negate_multiply_fusion
  340.7 7.1 %add_add_fusion.2 = f32[1536,768]{1,0:T(8,128)} fusion(f32[1536,768]{1,0:T(8,128)} %get-tuple-element.25, bf16[1536,768]{1,0:T(8,128)(2,1)} %param.18, f32[1536]{0:T(1024)S(1)} %negate_multiply_fusion, f32[1536]{0:T(1024)} %copy-done.30, f32[1536]{0:T(1024)S(1)} %multiply_multiply_fusion.2, f32[1536]{0:T(1024)S(1)} %copy-done.25, ...), kind=kLoop, calls=%fused_computation.38 | loop fusion | flops 14155776 | bytes 18908160 | tf_op jit(solution)/shard_map/add | solution.py:502
  348.1 0.9 copy-done.21
  349.1 0.6 copy-done.12
  349.9 0.3 copy-done.11
  350.3 0.7 copy-done.9
  351.1 0.7 slice-done.6
  351.9 0.3 constant_dynamic-update-slice_fusion.10
  352.2 0.1 copy_dynamic-update-slice_fusion
  352.4 6.3 %pad.20 = bf16[32,304,768]{2,1,0:T(8,128)(2,1)} pad(bf16[32,289,768]{2,1,0:T(8,128)(2,1)S(1)} %copy_dynamic-update-slice_fusion, bf16[]{:T(256)} %constant.24.clone.1), padding=0_0x0_15x0_0 | pad | bytes 29147138 | tf_op jit(solution)/shard_map/jit(_pad)/pad | solution.py:387
  358.6 88.1 %shard_map.274 = f32[304,768]{1,0:T(8,128)S(1)} custom-call(bf16[2,2,2,2,2,304,768]{6,5,4,3,2,1,0:T(8,128)(2,1)} %bitcast.75), custom_call_target="tpu_custom_call" | custom-call | tf_op jit(solution)/shard_map/pallas_call | solution.py:313
  446.7 0.6 slice_bitcast_fusion.1
  447.3 0.6 slice_bitcast_fusion
  447.9 0.7 slice.273
  448.6 0.7 fusion.40
  449.3 0.7 pad_maximum_fusion.6
  450.0 0.7 pad_maximum_fusion.7
  (131 shorter events, 1.9 us)
Async XLA Ops:
  0.7 11.6 %copy-start.22 = (bf16[24,3072]{1,0:T(8,128)(2,1)S(1)}, bf16[24,3072]{1,0:T(8,128)(2,1)}, u32[]{:S(2)}) copy-start(bf16[24,3072]{1,0:T(8,128)(2,1)} %param.28) | copy-start | bytes 442372
  0.7 11.5 %copy-start.26 = (bf16[24,2304]{1,0:T(8,128)(2,1)S(1)}, bf16[24,2304]{1,0:T(8,128)(2,1)}, u32[]{:S(2)}) copy-start(bf16[24,2304]{1,0:T(8,128)(2,1)} %param.21) | copy-start | bytes 331780
  0.7 12.9 %copy-start.36 = (s32[6,256]{1,0:T(8,128)S(1)}, s32[6,256]{1,0:T(8,128)}, u32[]{:S(2)}) copy-start(s32[6,256]{1,0:T(8,128)} %param.17) | copy-start | bytes 18436
  0.7 11.6 %copy-start.23 = (bf16[96,768]{1,0:T(8,128)(2,1)S(1)}, bf16[96,768]{1,0:T(8,128)(2,1)}, u32[]{:S(2)}) copy-start(bf16[96,768]{1,0:T(8,128)(2,1)} %param.30) | copy-start | bytes 442372
  0.7 11.5 %copy-start.35 = (bf16[24,768]{1,0:T(8,128)(2,1)S(1)}, bf16[24,768]{1,0:T(8,128)(2,1)}, u32[]{:S(2)}) copy-start(bf16[24,768]{1,0:T(8,128)(2,1)} %param.24) | copy-start | bytes 110596
  9.6 114.2 %copy-start.24 = (f32[1536]{0:T(1024)}, f32[1536]{0:T(1024)S(1)}, u32[]{:S(2)}) copy-start(f32[1536]{0:T(1024)S(1)} %broadcast_multiply_fusion.1) | copy-start | bytes 18436
  12.1 0.6 copy-start.31
  12.2 111.7 %copy-start.28 = (f32[1536]{0:T(1024)}, f32[1536]{0:T(1024)S(1)}, u32[]{:S(2)}) copy-start(f32[1536]{0:T(1024)S(1)} %fusion.24) | copy-start | bytes 18436
  13.8 117.6 %copy-start.3 = (s32[6,256,1]{2,1,0:T(8,128)}, s32[6,256,1]{2,1,0:T(8,128)S(1)}, u32[]{:S(2)}) copy-start(s32[6,256,1]{2,1,0:T(8,128)S(1)} %copy.32.row_ref) | copy-start | bytes 18436
  111.4 12.5 %copy-start.33 = (f32[768]{0:T(1024)}, f32[768]{0:T(1024)S(1)}, u32[]{:S(2)}) copy-start(f32[768]{0:T(1024)S(1)} %reshape.308) | copy-start | bytes 9220
  111.7 12.2 %copy-start.37 = (f32[768]{0:T(1024)}, f32[768]{0:T(1024)S(1)}, u32[]{:S(2)}) copy-start(f32[768]{0:T(1024)S(1)} %reshape.309) | copy-start | bytes 9220
  116.8 8.5 %copy-start.5 = (bf16[1536,768]{1,0:T(8,128)(2,1)S(1)}, bf16[1536,768]{1,0:T(8,128)(2,1)}, u32[]{:S(2)}) copy-start(bf16[1536,768]{1,0:T(8,128)(2,1)} %param.16) | copy-start | bytes 7077892
  123.8 1.0 copy-start.16
  123.8 1.4 copy-start.18
  123.8 7.6 %copy-start.19 = (bf16[32,24,768]{2,1,0:T(8,128)(2,1)}, bf16[32,24,768]{2,1,0:T(8,128)(2,1)S(1)}, u32[]{:S(2)}) copy-start(bf16[32,24,768]{2,1,0:T(8,128)(2,1)S(1)} %get-tuple-element.33) | copy-start | bytes 3538948
  131.5 15.3 %copy-start = (bf16[1536,2304]{1,0:T(8,128)(2,1)}, bf16[1536,2304]{1,0:T(8,128)(2,1)S(1)}, u32[]{:S(2)}) copy-start(bf16[1536,2304]{1,0:T(8,128)(2,1)S(1)} %add_convert_fusion.qkv_ref) | copy-start | bytes 21233668
  131.5 15.3 %copy-start.20 = (bf16[32,24,768]{2,1,0:T(8,128)(2,1)S(1)}, bf16[32,24,768]{2,1,0:T(8,128)(2,1)}, u32[]{:S(2)}) copy-start(bf16[32,24,768]{2,1,0:T(8,128)(2,1)} %get-tuple-element.30) | copy-start | bytes 3538948
  149.2 2.2 copy-start.7
  152.1 50.4 %slice-start.2 = ((s8[4718592]{0:T(1024)(128)(4,1)}), s8[524288]{0:T(1024)(128)(4,1)S(1)}, s32[]{:S(2)}) async-start(s8[4718592]{0:T(1024)(128)(4,1)} %bitcast.79), calls=%async_computation.2 | async-start | bytes 1048576
  174.0 28.4 %slice-start.3 = ((s8[4718592]{0:T(1024)(128)(4,1)}), s8[4194304]{0:T(1024)(128)(4,1)S(1)}, s32[]{:S(2)}) async-start(s8[4718592]{0:T(1024)(128)(4,1)} %bitcast.79), calls=%async_computation.3 | async-start | bytes 8388608
  174.0 28.4 %copy-start.39 = (bf16[1536,3072]{1,0:T(8,128)(2,1)S(1)}, bf16[1536,3072]{1,0:T(8,128)(2,1)}, u32[]{:S(2)}) copy-start(bf16[1536,3072]{1,0:T(8,128)(2,1)} %get-tuple-element.70) | copy-start | bytes 28311556
  202.5 11.2 %copy-start.8 = (bf16[1536,768]{1,0:T(8,128)(2,1)S(1)}, bf16[1536,768]{1,0:T(8,128)(2,1)}, u32[]{:S(2)}) copy-start(bf16[1536,768]{1,0:T(8,128)(2,1)} %param.18) | copy-start | bytes 7077892
  213.7 26.0 %slice-start.4 = ((s8[4718592]{0:T(1024)(128)(4,1)}), s8[524288]{0:T(1024)(128)(4,1)S(1)}, s32[]{:S(2)}) async-start(s8[4718592]{0:T(1024)(128)(4,1)} %bitcast.81), calls=%async_computation.4 | async-start | bytes 1048576
  224.3 15.3 %slice-start.5 = ((s8[4718592]{0:T(1024)(128)(4,1)}), s8[4194304]{0:T(1024)(128)(4,1)S(1)}, s32[]{:S(2)}) async-start(s8[4718592]{0:T(1024)(128)(4,1)} %bitcast.81), calls=%async_computation.5 | async-start | bytes 8388608
  254.6 3.7 copy-start.30
  263.1 3.1 copy-start.15
  266.9 4.9 %slice-start = ((s8[7077888]{0:T(1024)(128)(4,1)}), s8[2883584]{0:T(1024)(128)(4,1)S(1)}, s32[]{:S(2)}) async-start(s8[7077888]{0:T(1024)(128)(4,1)} %bitcast.73), calls=%async_computation | async-start | bytes 5767168
  267.6 4.2 slice-start.1
  267.6 4.2 copy-start.4
  299.0 2.9 copy-start.1
  301.9 8.2 %copy-start.6 = (bf16[1536,768]{1,0:T(8,128)(2,1)S(1)}, bf16[1536,768]{1,0:T(8,128)(2,1)}, u32[]{:S(2)}) copy-start(bf16[1536,768]{1,0:T(8,128)(2,1)} %param.16) | copy-start | bytes 7077892
  301.9 8.2 %copy-start.17 = (bf16[32,24,768]{2,1,0:T(8,128)(2,1)S(1)}, bf16[32,24,768]{2,1,0:T(8,128)(2,1)}, u32[]{:S(2)}) copy-start(bf16[32,24,768]{2,1,0:T(8,128)(2,1)} %copy-done.16) | copy-start | bytes 3538948
  301.9 8.2 %copy-start.25 = (f32[1536]{0:T(1024)S(1)}, f32[1536]{0:T(1024)}, u32[]{:S(2)}) copy-start(f32[1536]{0:T(1024)} %copy-done.24) | copy-start | bytes 18436
  301.9 8.2 %copy-start.34 = (f32[768]{0:T(1024)S(1)}, f32[768]{0:T(1024)}, u32[]{:S(2)}) copy-start(f32[768]{0:T(1024)} %copy-done.33) | copy-start | bytes 9220
  310.0 12.6 %copy-start.2 = (bf16[1536,2304]{1,0:T(8,128)(2,1)S(1)}, bf16[1536,2304]{1,0:T(8,128)(2,1)}, u32[]{:S(2)}) copy-start(bf16[1536,2304]{1,0:T(8,128)(2,1)} %copy-done.1) | copy-start | bytes 21233668
  310.0 12.6 %copy-start.29 = (f32[1536]{0:T(1024)S(1)}, f32[1536]{0:T(1024)}, u32[]{:S(2)}) copy-start(f32[1536]{0:T(1024)} %copy-done.28) | copy-start | bytes 18436
  310.1 12.6 %copy-start.38 = (f32[768]{0:T(1024)S(1)}, f32[768]{0:T(1024)}, u32[]{:S(2)}) copy-start(f32[768]{0:T(1024)} %copy-done.37) | copy-start | bytes 9220
  322.7 6.7 %copy-start.32 = (f32[1536]{0:T(1024)S(1)}, f32[1536]{0:T(1024)}, u32[]{:S(2)}) copy-start(f32[1536]{0:T(1024)} %copy-done.31) | copy-start | bytes 18436
  340.7 7.1 %copy-start.27 = (bf16[32,288]{1,0:T(8,128)(2,1)S(1)}, bf16[32,288]{1,0:T(8,128)(2,1)}, u32[]{:S(2)}) copy-start(bf16[32,288]{1,0:T(8,128)(2,1)} %concatenate.33) | copy-start | bytes 55300
  340.7 7.1 %copy-start.14 = (bf16[768,768]{1,0:T(8,128)(2,1)S(1)}, bf16[768,768]{1,0:T(8,128)(2,1)}, u32[]{:S(2)}) copy-start(bf16[768,768]{1,0:T(8,128)(2,1)} %get-tuple-element.40) | copy-start | bytes 3538948
  340.7 7.2 %copy-start.13 = (bf16[768,768]{1,0:T(8,128)(2,1)S(1)}, bf16[768,768]{1,0:T(8,128)(2,1)}, u32[]{:S(2)}) copy-start(bf16[768,768]{1,0:T(8,128)(2,1)} %get-tuple-element.39) | copy-start | bytes 3538948
  347.8 1.3 copy-start.21
  347.8 2.0 copy-start.12
  347.9 2.2 copy-start.11
  347.9 3.9 slice-start.6
  348.0 2.2 copy-start.10
  349.1 2.0 copy-start.9
  349.8 2.1 slice-start.7
